TPU v7x, 768 devices: a whole 4x8x12 slice. The times are simulated.
768 devices in a mesh: mesh: 96 (over z, x, core), sub: 8 (over y).
Axes of the slice: x: 4, y: 8, z: 12, core: 2. Of those that a mesh axis runs over, the one named last changes fastest.
Arguments:
- state: float32 [56, 9, 98304], P(None, None, ('mesh', 'sub')), may hold values from -6 to 6
- scales: float32 [98304], P(('mesh', 'sub')), may hold values from 0.5 to 2
- stiffness: float32 [3, 56, 56], replicated, may hold values from -0.75 to 0.75
- jacobians: float32 [3, 9, 9], replicated, may hold values from -2 to 2
- projection: float32 [4, 21, 56], replicated, may hold values from -0.75 to 0.75
- lifting: float32 [4, 56, 21], replicated, may hold values from -1.25 to 1.25
- flux_matrix: float32 [9, 9], replicated, may hold values from -2 to 2
- peer_send: int32 [768, 8, 8], P(('mesh', 'sub')), may hold values from -1 to 511, as said below
- peer_recv: int32 [768, 8, 8], P(('mesh', 'sub')), may hold values from -1 to 511, as said below
- edge_send: int32 [768, 2, 32], P(('mesh', 'sub')), may hold values from -1 to 511, as said below
- edge_recv: int32 [768, 2, 32], P(('mesh', 'sub')), may hold values from -1 to 511, as said below
- uplift_map: float32 [504, 256], replicated, may hold values from -0.25 to 0.25
- fault_elem: int32 [49152], P(('mesh', 'sub')), may hold values from 0 to 127
- fault_dest: int32 [49152, 1], P(('mesh', 'sub')), may hold values from 0 to 7; in each aligned block of 64 rows (0 to 63, 64 to 127, ...) at most 16 rows name the same one
- fault_row: int32 [49152], P(('mesh', 'sub')), may hold values from 0 to 63
- fault_slip: int32 [49152], P(('mesh', 'sub')), may hold values 0 or 1
- sea_level: float32 [6144, 2048], P('mesh', 'sub'), may hold values from -6 to 6
- velocity: float32 [2, 6144, 2048], P(None, 'mesh', 'sub'), may hold values from -4 to 4
- depth: float32 [6144, 2048], P('mesh', 'sub'), may hold values from 0.5 to 2
Outputs:
- new_state: float32 [56, 9, 98304], P(None, None, ('mesh', 'sub'))
- sea_out: float32 [6144, 2048], P('mesh', 'sub')
- flow_out: float32 [2, 6144, 2048], P(None, 'mesh', 'sub')
Inputs may be any that keep to these rules, and one draw needn't show every extreme that they name: `peer_send`: entry [d, p, j] is a face code of device d, or -1 for a padded slot; live slots come first in each block. Block [(m, s), p] holds as many live slots as block [(m, p), s] of peer_recv, and the block with p = s is full. `peer_recv`: entry [d, p, j] is a face code of device d, or -1 for a padded slot; live slots come first in each block, as many as in block [(m, p), s] of peer_send for d = (m, s). `edge_send`: entry [d, side, j] is a face code of device d, or -1 for a padded slot; live slots come first. Block [(m, s), 1] holds as many live slots as block [(m + 1, s), 0] of edge_recv, block [(m, s), 0] as many as block [(m - 1, s), 1] of edge_recv; blocks towards a missing neighbour are all -1. Block [(0, s), 1] is full. `edge_recv`: entry [d, side, j] is a face code of device d, or -1 for a padded slot; live slots come first, as many as in the matching block of edge_send. `fault_dest`: among the 64 fault faces of one device, at most 16 name the same column.
All inputs are finite; a program needn't handle non-finite values. No bound on the sum of `fault_slip` on one device may be relied on, other than what follows from the above.
Results may differ from a plain program's by a relative error of at most 0.0003.
Values sent between devices are 32-bit elements; how exact they have to be, the bound alone decides.
A program may use at most 64 MiB of HBM per device.

v0:
```python
import jax
import jax.numpy as jnp
from jax import lax
from jax.sharding import PartitionSpec as P

ORDER = 5
CAP = 16
SEA_STEPS = 2


EXACT_PRECISION = lax.Precision.HIGHEST
EARTH_STEP = 0.5
COURANT = 0.45


def padded_2(array, sides, width):
    for axis, dim in sides:
        count, length = (lax.axis_size(axis), array.shape[dim])
        up = [(i, (i + 1) % count) for i in range(count - 1)]
        down = [(j, i) for i, j in up]
        last = lax.slice_in_dim(array, length - width, length, axis=dim)
        first = lax.slice_in_dim(array, 0, width, axis=dim)
        before = lax.ppermute(last, axis, up)
        after = lax.ppermute(first, axis, down)
        array = jnp.concatenate([before, array, after], axis=dim)
    return array


def derivative(field_in, scales, stiffness, jacobians):
    summed = jnp.zeros(field_in.shape, jnp.float32)
    for direction in range(3):
        basis_mixed = jnp.einsum(
            "cb,bqe->cqe", stiffness[direction], field_in, precision=EXACT_PRECISION
        )
        summed = summed + jnp.einsum(
            "cpe,pq->cqe", basis_mixed, jacobians[direction], precision=EXACT_PRECISION
        )
    return summed * scales


def predictor(field_in, scales, stiffness, jacobians):
    factor = EARTH_STEP
    integral = factor * field_in
    current = field_in
    for power in range(1, ORDER):
        current = derivative(current, scales, stiffness, jacobians)
        factor = factor * EARTH_STEP / (power + 1)
        integral = integral + factor * current
    return integral


def face_select(face_codes):
    live_slot = face_codes >= 0
    element = jnp.where(live_slot, face_codes // 4, 0)
    select = ((face_codes % 4)[None, :] == jnp.arange(4, dtype=jnp.int32)[:, None]) & live_slot[
        None, :
    ]
    return (element, select.astype(jnp.float32))


def project_faces(picked, select, projection):
    chosen_proj = jnp.einsum("fnb,fm->nbm", projection, select, precision=EXACT_PRECISION)
    return jnp.einsum("nbm,bqm->nqm", chosen_proj, picked, precision=EXACT_PRECISION)


def traces(integral, face_codes, projection):
    element, select = face_select(face_codes)
    picked = jnp.take(integral, element, axis=2)
    return project_faces(picked, select, projection)


def face_terms(integral, incoming, face_codes, projection, lifting, flux_matrix, element_count):
    element, select = face_select(face_codes)
    own_trace = traces(integral, face_codes, projection)
    face_flux = jnp.einsum(
        "npm,pq->nqm", incoming - own_trace, flux_matrix, precision=EXACT_PRECISION
    )
    chosen_lift = jnp.einsum("fbn,fm->bnm", lifting, select, precision=EXACT_PRECISION)
    lifted = jnp.einsum("bnm,nqm->bqm", chosen_lift, face_flux, precision=EXACT_PRECISION)
    empty_sum = jnp.zeros((integral.shape[0], integral.shape[1], element_count), jnp.float32)
    return empty_sum.at[:, :, element].add(lifted)


def advance(padded, sea_flow):
    height_pad = padded[0]
    flux_rows = padded[1]
    flux_cols = padded[2]
    divergence = (flux_rows[2:, 1:-1] - flux_rows[:-2, 1:-1]) * 0.5 + (
        flux_cols[1:-1, 2:] - flux_cols[1:-1, :-2]
    ) * 0.5
    height_cycle = height_pad[1:-1, 1:-1] - COURANT * divergence
    slope_rows = (height_cycle[2:, 1:-1] - height_cycle[:-2, 1:-1]) * 0.5
    slope_cols = (height_cycle[1:-1, 2:] - height_cycle[1:-1, :-2]) * 0.5
    new_flow = sea_flow - COURANT * jnp.stack([slope_rows, slope_cols])
    return (height_cycle[1:-1, 1:-1], new_flow)


def body(
    state,
    scales,
    stiffness,
    jacobians,
    projection,
    lifting,
    flux_matrix,
    peer_send,
    peer_recv,
    edge_send,
    edge_recv,
    uplift_map,
    fault_elem,
    fault_dest,
    fault_row,
    fault_slip,
    sea_level,
    velocity,
    depth,
):
    sub_count = lax.axis_size("sub")
    basis_count = state.shape[0]
    quantity_count = state.shape[1]
    face_basis = projection.shape[1]
    column_width = basis_count * quantity_count
    trace_width = face_basis * quantity_count
    elements = state.shape[2]
    peer_slots = peer_send.shape[2]
    edge_slots = edge_send.shape[2]
    peer_total = sub_count * peer_slots
    tile_rows = sea_level.shape[0]
    send_codes = jnp.concatenate([peer_send.reshape(-1), edge_send.reshape(-1)])
    recv_codes = jnp.concatenate([peer_recv.reshape(-1), edge_recv.reshape(-1)])
    integral = predictor(state, scales, stiffness, jacobians)
    outgoing = traces(integral, send_codes, projection).reshape(trace_width, -1)
    got_peer = lax.all_to_all(
        outgoing[:, :peer_total].reshape(trace_width, sub_count, peer_slots),
        "sub",
        split_axis=1,
        concat_axis=1,
        tiled=True,
    )
    edge_rim = padded_2(
        outgoing[:, peer_total:].reshape(trace_width, 2, edge_slots), (("mesh", 1),), 1
    )
    incoming = jnp.concatenate(
        [got_peer.reshape(trace_width, peer_total), edge_rim[:, 0], edge_rim[:, 3]], 1
    )
    incoming = incoming.reshape(face_basis, quantity_count, -1)
    volume = derivative(integral, scales, stiffness, jacobians)
    face_sum = face_terms(
        integral, incoming, recv_codes, projection, lifting, flux_matrix, elements
    )
    new_state = state + volume + face_sum
    fault_columns = jnp.take(new_state, fault_elem, axis=2).reshape(column_width, -1)
    weighting = 0.3 + 0.7 * fault_slip.astype(jnp.float32)
    uplift_items = (
        jnp.einsum("kf,kt->ft", fault_columns, uplift_map, precision=EXACT_PRECISION)
        * weighting[:, None]
    )
    target = fault_dest[:, 0]
    dest_hits = (target[:, None] == jnp.arange(sub_count, dtype=jnp.int32)[None, :]).astype(
        jnp.int32
    )
    before = jnp.sum((jnp.cumsum(dest_hits, 0) - dest_hits) * dest_hits, 1)
    slot_index = target * CAP + before
    placing = (slot_index[None, :] == jnp.arange(sub_count * CAP, dtype=jnp.int32)[:, None]).astype(
        jnp.float32
    )
    packed = jnp.dot(placing, uplift_items, precision=EXACT_PRECISION)
    packed_row = jnp.dot(placing, fault_row.astype(jnp.float32), precision=EXACT_PRECISION)
    got_rows, got_index = (
        lax.all_to_all(
            packed.reshape(sub_count, CAP, -1), "sub", split_axis=0, concat_axis=0, tiled=True
        ),
        lax.all_to_all(
            packed_row.reshape(sub_count, CAP), "sub", split_axis=0, concat_axis=0, tiled=True
        ),
    )
    landing = (
        got_index.reshape(-1)[None, :] == jnp.arange(tile_rows, dtype=jnp.float32)[:, None]
    ).astype(jnp.float32)
    deposit = jnp.dot(landing, got_rows.reshape(sub_count * CAP, -1), precision=EXACT_PRECISION)
    sea_height = sea_level + deposit
    sea_flow = velocity
    for substep in range(SEA_STEPS):
        stacked = jnp.concatenate([sea_height[None], depth[None] * sea_flow], 0)
        padded = padded_2(stacked, (("mesh", 1), ("sub", 2)), 2)
        sea_height, sea_flow = advance(padded, sea_flow)
    return (new_state, sea_height, sea_flow)


def solution(mesh):
    return jax.shard_map(
        body,
        mesh=mesh,
        in_specs=(
            P(None, None, ("mesh", "sub")),
            P(("mesh", "sub")),
            P(),
            P(),
            P(),
            P(),
            P(),
            P(("mesh", "sub"), None, None),
            P(("mesh", "sub"), None, None),
            P(("mesh", "sub"), None, None),
            P(("mesh", "sub"), None, None),
            P(),
            P(("mesh", "sub")),
            P(("mesh", "sub"), None),
            P(("mesh", "sub")),
            P(("mesh", "sub")),
            P("mesh", "sub"),
            P(None, "mesh", "sub"),
            P("mesh", "sub"),
        ),
        out_specs=(P(None, None, ("mesh", "sub")), P("mesh", "sub"), P(None, "mesh", "sub")),
        check_vma=False,
    )
```

profile of v0, /device:TPU:199, one launch (start us, length us, event | category | flops | bytes accessed | tf_op | source)
XLA Modules:
  0.0 166.0 jit_solution(16571950070648213488)
XLA Ops:
  19.6 2.8 %gather_fusion.1 = f32[128,56,9]{1,2,0:T(8,128)} fusion(f32[56,9,128]{0,1,2:T(8,128)} %copy.260, s32[1024]{0:T(1024)S(1)} %pad_clamp_fusion.2), kind=kCustom, calls=%fused_computation.clone | custom fusion | bytes 516608 | tf_op jit(solution)/shard_map/jit(_take)/gather | solution.py:68
  22.4 4.8 %convolution_bitcast_fusion.1 = f32[21,9,128]{0,1,2:T(8,128)} fusion(f32[21,56,128]{1,0,2:T(8,128)S(1)} %copy.261, f32[128,56,9]{1,2,0:T(8,128)} %gather_fusion.1, pred[128]{0:T(512)(128)(4,1)S(1)} %get-tuple-element.22), kind=kOutput, calls=%fused_computation.5 | convolution fusion | flops 16321536 | bytes 957056 | tf_op jit(solution)/shard_map/nbm,bqm->nqm/dot_general | solution.py:63
  29.8 6.8 %all-to-all-start = ((f32[189,8,8]{0,2,1:T(8,128)}), f32[189,8,8]{0,2,1:T(8,128)}, u32[]{:S(2)}, u32[]{:S(2)}) async-start(f32[189,8,8]{0,2,1:T(8,128)} %bitcast.48), calls=%async_computation | async-start | bytes 131072 | tf_op jit(solution)/shard_map/all_to_all | solution.py:134
  37.3 6.0 %collective-permute-start = (f32[189,1,32]{0,2,1:T(8,128)}, f32[189,1,32]{0,2,1:T(8,128)}, u32[]{:S(2)}, u32[]{:S(2)}) collective-permute-start(f32[189,1,32]{0,2,1:T(8,128)} %get-tuple-element.47), channel_id=1, source_target_pairs={{0,8},{8,16},{16,24},{24,32},{32,40},{40,48},{48,56},{56,64},{64,7... | collective-permute-start | bytes 72584 | tf_op jit(solution)/shard_map/ppermute | solution.py:23
  43.3 1.9 %collective-permute-start.1 = (f32[189,1,32]{0,2,1:T(8,128)S(1)}, f32[189,1,32]{0,2,1:T(8,128)S(1)}, u32[]{:S(2)}, u32[]{:S(2)}) collective-permute-start(f32[189,1,32]{0,2,1:T(8,128)S(1)} %get-tuple-element.48), channel_id=1, source_target_pairs={{8,0},{16,8},{24,16},{32,24},{40,32},{48,40},{56,48},{64,56},{72,6... | collective-permute-start | bytes 72584 | tf_op jit(solution)/shard_map/ppermute | solution.py:24
  55.5 2.9 %gather_fusion.2 = f32[128,56,9]{1,2,0:T(8,128)} fusion(f32[56,9,128]{0,1,2:T(8,128)} %copy.260, s32[1024]{0:T(1024)S(1)} %pad_clamp_fusion.1), kind=kCustom, calls=%fused_computation.1.clone | custom fusion | bytes 516608 | tf_op jit(solution)/shard_map/jit(_take)/gather | solution.py:68
  67.0 6.9 %all-to-all-start.1 = ((f32[8,1,16]{2,1,0:T(1,128)}), f32[8,1,16]{2,1,0:T(1,128)S(1)}, u32[]{:S(2)}, u32[]{:S(2)}) async-start(f32[8,1,16]{2,1,0:T(1,128)} %bitcast.58), calls=%async_computation.1 | async-start | bytes 8192 | tf_op jit(solution)/shard_map/all_to_all | solution.py:174
  73.9 2.0 %concatenate.103 = f32[21,9,64]{1,0,2:T(8,128)} reshape(f32[189,8,8]{0,2,1:T(8,128)} %all-to-all-done) | data formatting | bytes 96768 | tf_op jit(solution)/shard_map/concatenate | solution.py:144
  75.9 2.4 %copy.267 = f32[21,9,64]{0,1,2:T(8,128)} copy(f32[21,9,64]{1,0,2:T(8,128)} %concatenate.103) | data formatting | bytes 96768 | tf_op jit(solution)/shard_map/concatenate | solution.py:144
  78.3 5.6 %maximum_subtract_fusion = f32[21,9,128]{0,1,2:T(8,128)} fusion(f32[21,9,32]{0,1,2:T(8,128)} %copy.269, f32[21,9,32]{0,1,2:T(8,128)S(1)} %copy.268, f32[21,9,64]{0,1,2:T(8,128)} %copy.267, f32[21,56,128]{1,0,2:T(8,128)} %copy.271, f32[128,56,9]{1,2,0:T(8,128)} %gather_fusion.2, pred[128]{0:T(512)(128)(4,1)S(1)} %get-tuple-element.19), kind=kOutput, calls=%fused_computation.26 | convolution fusion | flops 16394112 | bytes 1053824 | tf_op jit(solution)/shard_map/nbm,bqm->nqm/dot_general | solution.py:63
  87.3 3.9 %fusion.137 = f32[128,56,9]{1,2,0:T(8,128)} fusion(f32[56,21,128]{0,1,2:T(8,128)S(1)} %copy.274, f32[9,21,128]{1,0,2:T(8,128)} %copy.275), kind=kOutput, calls=%fused_computation.241 | convolution fusion | flops 16257024 | bytes 956928 | tf_op jit(solution)/shard_map/bnm,nqm->bqm/dot_general | solution.py:79
  91.2 10.5 %scatter_fusion = f32[56,9,128]{0,1,2:T(8,128)S(1)} fusion(f32[56,9,128]{0,1,2:T(8,128)S(1)} %copy.276, s32[128]{0:T(128)S(1)} %copy-done.19, f32[128,56,9]{1,2,0:T(8,128)} %fusion.137), kind=kCustom, calls=%fused_computation.3 | custom fusion | flops 64512 | bytes 774656 | tf_op jit(solution)/shard_map/scatter-add | solution.py:81
  104.4 6.7 %all-to-all-start.2 = ((f32[8,16,256]{2,1,0:T(8,128)}), f32[8,16,256]{2,1,0:T(8,128)S(1)}, u32[]{:S(2)}, u32[]{:S(2)}) async-start(f32[8,16,256]{2,1,0:T(8,128)} %bitcast.60), calls=%async_computation.2 | async-start | bytes 262144 | tf_op jit(solution)/shard_map/all_to_all | solution.py:171
  112.3 8.3 %all-to-all-done.2 = f32[8,16,256]{2,1,0:T(8,128)S(1)} async-done(((f32[8,16,256]{2,1,0:T(8,128)}), f32[8,16,256]{2,1,0:T(8,128)S(1)}, u32[]{:S(2)}, u32[]{:S(2)}) %all-to-all-start.2) | async-done | bytes 131104 | tf_op jit(solution)/shard_map/all_to_all | solution.py:171
  120.8 7.3 %collective-permute-start.2 = (f32[3,2,256]{2,1,0:T(2,128)S(1)}, f32[3,2,256]{2,1,0:T(2,128)S(1)}, u32[]{:S(2)}, u32[]{:S(2)}) collective-permute-start(f32[3,2,256]{2,1,0:T(2,128)S(1)} %get-tuple-element.37), channel_id=1, source_target_pairs={{0,8},{8,16},{16,24},{24,32},{32,40},{40,48},{48,56},{56,64},{64,7... | collective-permute-start | bytes 18440 | tf_op jit(solution)/shard_map/ppermute | solution.py:23
  128.2 1.9 %collective-permute-start.3 = (f32[3,2,256]{2,1,0:T(2,128)S(1)}, f32[3,2,256]{2,1,0:T(2,128)S(1)}, u32[]{:S(2)}, u32[]{:S(2)}) collective-permute-start(f32[3,2,256]{2,1,0:T(2,128)S(1)} %get-tuple-element.38), channel_id=1, source_target_pairs={{8,0},{16,8},{24,16},{32,24},{40,32},{48,40},{56,48},{64,56},{72,6... | collective-permute-start | bytes 18440 | tf_op jit(solution)/shard_map/ppermute | solution.py:24
  130.1 6.3 %collective-permute-done.3 = f32[3,2,256]{2,1,0:T(2,128)S(1)} collective-permute-done((f32[3,2,256]{2,1,0:T(2,128)S(1)}, f32[3,2,256]{2,1,0:T(2,128)S(1)}, u32[]{:S(2)}, u32[]{:S(2)}) %collective-permute-start.3) | collective-permute-done | bytes 6176 | tf_op jit(solution)/shard_map/ppermute | solution.py:24
  136.6 2.2 %collective-permute-start.4 = (f32[3,68,2]{2,1,0:T(8,128)S(1)}, f32[3,68,2]{2,1,0:T(8,128)S(1)}, u32[]{:S(2)}, u32[]{:S(2)}) collective-permute-start(f32[3,68,2]{2,1,0:T(8,128)S(1)} %get-tuple-element.33), channel_id=1, source_target_pairs={{0,1},{1,2},{2,3},{3,4},{4,5},{5,6},{6,7},{8,9},{9,10},{10,11},{11... | collective-permute-start | bytes 4904 | tf_op jit(solution)/shard_map/ppermute | solution.py:23
  140.5 3.8 %collective-permute-done.5 = f32[3,68,2]{2,1,0:T(8,128)S(1)} collective-permute-done((f32[3,68,2]{2,1,0:T(8,128)S(1)}, f32[3,68,2]{2,1,0:T(8,128)S(1)}, u32[]{:S(2)}, u32[]{:S(2)}) %collective-permute-start.5) | collective-permute-done | bytes 1664 | tf_op jit(solution)/shard_map/ppermute | solution.py:24
  144.9 3.4 %collective-permute-start.6 = (f32[3,2,256]{2,1,0:T(2,128)S(1)}, f32[3,2,256]{2,1,0:T(2,128)S(1)}, u32[]{:S(2)}, u32[]{:S(2)}) collective-permute-start(f32[3,2,256]{2,1,0:T(2,128)S(1)} %get-tuple-element.35), channel_id=1, source_target_pairs={{0,8},{8,16},{16,24},{24,32},{32,40},{40,48},{48,56},{56,64},{64,7... | collective-permute-start | bytes 18440 | tf_op jit(solution)/shard_map/ppermute | solution.py:23
  148.2 1.9 %collective-permute-start.7 = (f32[3,2,256]{2,1,0:T(2,128)S(1)}, f32[3,2,256]{2,1,0:T(2,128)S(1)}, u32[]{:S(2)}, u32[]{:S(2)}) collective-permute-start(f32[3,2,256]{2,1,0:T(2,128)S(1)} %get-tuple-element.36), channel_id=1, source_target_pairs={{8,0},{16,8},{24,16},{32,24},{40,32},{48,40},{56,48},{64,56},{72,6... | collective-permute-start | bytes 18440 | tf_op jit(solution)/shard_map/ppermute | solution.py:24
  150.2 6.3 %collective-permute-done.7 = f32[3,2,256]{2,1,0:T(2,128)S(1)} collective-permute-done((f32[3,2,256]{2,1,0:T(2,128)S(1)}, f32[3,2,256]{2,1,0:T(2,128)S(1)}, u32[]{:S(2)}, u32[]{:S(2)}) %collective-permute-start.7) | collective-permute-done | bytes 6176 | tf_op jit(solution)/shard_map/ppermute | solution.py:24
  156.6 2.0 %collective-permute-start.8 = (f32[3,68,2]{2,1,0:T(8,128)S(1)}, f32[3,68,2]{2,1,0:T(8,128)S(1)}, u32[]{:S(2)}, u32[]{:S(2)}) collective-permute-start(f32[3,68,2]{2,1,0:T(8,128)S(1)} %get-tuple-element.31), channel_id=1, source_target_pairs={{0,1},{1,2},{2,3},{3,4},{4,5},{5,6},{6,7},{8,9},{9,10},{10,11},{11... | collective-permute-start | bytes 4904 | tf_op jit(solution)/shard_map/ppermute | solution.py:23
  161.0 3.2 %collective-permute-done.9 = f32[3,68,2]{2,1,0:T(8,128)S(1)} collective-permute-done((f32[3,68,2]{2,1,0:T(8,128)S(1)}, f32[3,68,2]{2,1,0:T(8,128)S(1)}, u32[]{:S(2)}, u32[]{:S(2)}) %collective-permute-start.9) | collective-permute-done | bytes 1664 | tf_op jit(solution)/shard_map/ppermute | solution.py:24
  (173 shorter events, 54.6 us)
Async XLA Ops:
  0.6 102.2 %copy-start = (f32[504,256]{1,0:T(8,128)S(1)}, f32[504,256]{1,0:T(8,128)}, u32[]{:S(2)}) copy-start(f32[504,256]{1,0:T(8,128)} %param.32) | copy-start | bytes 1548292
  0.6 4.1 %copy-start.10 = (f32[3,9,9]{2,0,1:T(4,128)S(1)}, f32[3,9,9]{2,0,1:T(4,128)}, u32[]{:S(2)}) copy-start(f32[3,9,9]{2,0,1:T(4,128)} %param.24) | copy-start | bytes 2920
  27.2 18.0 %copy-start.8 = (s32[1,8,8]{2,1,0:T(8,128)S(1)}, s32[1,8,8]{2,1,0:T(8,128)}, u32[]{:S(2)}) copy-start(s32[1,8,8]{2,1,0:T(8,128)} %param.29) | copy-start | bytes 772
  27.2 18.1 %copy-start.21 = (s32[1,2,32]{2,1,0:T(2,128)S(1)}, s32[1,2,32]{2,1,0:T(2,128)}, u32[]{:S(2)}) copy-start(s32[1,2,32]{2,1,0:T(2,128)} %param.31) | copy-start | bytes 772
  28.9 19.0 %copy-start.22 = (s32[64]{0:T(128)S(1)}, s32[64]{0:T(128)}, u32[]{:S(2)}) copy-start(s32[64]{0:T(128)} %param.33) | copy-start | bytes 772
  29.0 19.7 %copy-start.7 = (f32[4,56,21]{1,0,2:T(4,128)S(1)}, f32[4,56,21]{1,0,2:T(4,128)}, u32[]{:S(2)}) copy-start(f32[4,56,21]{1,0,2:T(4,128)} %param.26) | copy-start | bytes 56452
  29.8 37.2 %all-to-all-start = ((f32[189,8,8]{0,2,1:T(8,128)}), f32[189,8,8]{0,2,1:T(8,128)}, u32[]{:S(2)}, u32[]{:S(2)}) async-start(f32[189,8,8]{0,2,1:T(8,128)} %bitcast.48), calls=%async_computation | async-start | bytes 131072 | tf_op jit(solution)/shard_map/all_to_all | solution.py:134
  37.3 24.4 %collective-permute-start = (f32[189,1,32]{0,2,1:T(8,128)}, f32[189,1,32]{0,2,1:T(8,128)}, u32[]{:S(2)}, u32[]{:S(2)}) collective-permute-start(f32[189,1,32]{0,2,1:T(8,128)} %get-tuple-element.47), channel_id=1, source_target_pairs={{0,8},{8,16},{16,24},{24,32},{32,40},{40,48},{48,56},{56,64},{64,7... | collective-permute-start | bytes 72584 | tf_op jit(solution)/shard_map/ppermute | solution.py:23
  43.3 21.1 %collective-permute-start.1 = (f32[189,1,32]{0,2,1:T(8,128)S(1)}, f32[189,1,32]{0,2,1:T(8,128)S(1)}, u32[]{:S(2)}, u32[]{:S(2)}) collective-permute-start(f32[189,1,32]{0,2,1:T(8,128)S(1)} %get-tuple-element.48), channel_id=1, source_target_pairs={{8,0},{16,8},{24,16},{32,24},{40,32},{48,40},{56,48},{64,56},{72,6... | collective-permute-start | bytes 72584 | tf_op jit(solution)/shard_map/ppermute | solution.py:24
  52.9 5.5 %copy-start.15 = (s32[64]{0:T(128)}, s32[64]{0:T(128)S(1)}, u32[]{:S(2)}) copy-start(s32[64]{0:T(128)S(1)} %multiply_add_fusion.1) | copy-start | bytes 772
  67.0 37.4 %all-to-all-start.1 = ((f32[8,1,16]{2,1,0:T(1,128)}), f32[8,1,16]{2,1,0:T(1,128)S(1)}, u32[]{:S(2)}, u32[]{:S(2)}) async-start(f32[8,1,16]{2,1,0:T(1,128)} %bitcast.58), calls=%async_computation.1 | async-start | bytes 8192 | tf_op jit(solution)/shard_map/all_to_all | solution.py:174
  78.3 7.2 %copy-start.11 = (f32[9,9]{1,0:T(8,128)S(1)}, f32[9,9]{1,0:T(8,128)}, u32[]{:S(2)}) copy-start(f32[9,9]{1,0:T(8,128)} %param.27) | copy-start | bytes 976
  102.4 8.6 %copy-start.3 = (f32[2,64,256]{2,1,0:T(8,128)S(1)}, f32[2,64,256]{2,1,0:T(8,128)}, u32[]{:S(2)}) copy-start(f32[2,64,256]{2,1,0:T(8,128)} %param.38) | copy-start | bytes 393220
  102.4 8.6 %copy-start.4 = (f32[64,256]{1,0:T(8,128)S(1)}, f32[64,256]{1,0:T(8,128)}, u32[]{:S(2)}) copy-start(f32[64,256]{1,0:T(8,128)} %param.39) | copy-start | bytes 196612
  102.5 18.2 %copy-start.6 = (f32[64,256]{1,0:T(8,128)S(1)}, f32[64,256]{1,0:T(8,128)}, u32[]{:S(2)}) copy-start(f32[64,256]{1,0:T(8,128)} %param.37) | copy-start | bytes 196612
  104.4 16.3 %all-to-all-start.2 = ((f32[8,16,256]{2,1,0:T(8,128)}), f32[8,16,256]{2,1,0:T(8,128)S(1)}, u32[]{:S(2)}, u32[]{:S(2)}) async-start(f32[8,16,256]{2,1,0:T(8,128)} %bitcast.60), calls=%async_computation.2 | async-start | bytes 262144 | tf_op jit(solution)/shard_map/all_to_all | solution.py:171
  120.8 9.3 %collective-permute-start.2 = (f32[3,2,256]{2,1,0:T(2,128)S(1)}, f32[3,2,256]{2,1,0:T(2,128)S(1)}, u32[]{:S(2)}, u32[]{:S(2)}) collective-permute-start(f32[3,2,256]{2,1,0:T(2,128)S(1)} %get-tuple-element.37), channel_id=1, source_target_pairs={{0,8},{8,16},{16,24},{24,32},{32,40},{40,48},{48,56},{56,64},{64,7... | collective-permute-start | bytes 18440 | tf_op jit(solution)/shard_map/ppermute | solution.py:23
  128.2 8.3 %collective-permute-start.3 = (f32[3,2,256]{2,1,0:T(2,128)S(1)}, f32[3,2,256]{2,1,0:T(2,128)S(1)}, u32[]{:S(2)}, u32[]{:S(2)}) collective-permute-start(f32[3,2,256]{2,1,0:T(2,128)S(1)} %get-tuple-element.38), channel_id=1, source_target_pairs={{8,0},{16,8},{24,16},{32,24},{40,32},{48,40},{56,48},{64,56},{72,6... | collective-permute-start | bytes 18440 | tf_op jit(solution)/shard_map/ppermute | solution.py:24
  136.6 3.9 %collective-permute-start.4 = (f32[3,68,2]{2,1,0:T(8,128)S(1)}, f32[3,68,2]{2,1,0:T(8,128)S(1)}, u32[]{:S(2)}, u32[]{:S(2)}) collective-permute-start(f32[3,68,2]{2,1,0:T(8,128)S(1)} %get-tuple-element.33), channel_id=1, source_target_pairs={{0,1},{1,2},{2,3},{3,4},{4,5},{5,6},{6,7},{8,9},{9,10},{10,11},{11... | collective-permute-start | bytes 4904 | tf_op jit(solution)/shard_map/ppermute | solution.py:23
  138.8 5.5 %collective-permute-start.5 = (f32[3,68,2]{2,1,0:T(8,128)S(1)}, f32[3,68,2]{2,1,0:T(8,128)S(1)}, u32[]{:S(2)}, u32[]{:S(2)}) collective-permute-start(f32[3,68,2]{2,1,0:T(8,128)S(1)} %get-tuple-element.34), channel_id=1, source_target_pairs={{1,0},{2,1},{3,2},{4,3},{5,4},{6,5},{7,6},{9,8},{10,9},{11,10},{12... | collective-permute-start | bytes 4904 | tf_op jit(solution)/shard_map/ppermute | solution.py:24
  144.9 5.3 %collective-permute-start.6 = (f32[3,2,256]{2,1,0:T(2,128)S(1)}, f32[3,2,256]{2,1,0:T(2,128)S(1)}, u32[]{:S(2)}, u32[]{:S(2)}) collective-permute-start(f32[3,2,256]{2,1,0:T(2,128)S(1)} %get-tuple-element.35), channel_id=1, source_target_pairs={{0,8},{8,16},{16,24},{24,32},{32,40},{40,48},{48,56},{56,64},{64,7... | collective-permute-start | bytes 18440 | tf_op jit(solution)/shard_map/ppermute | solution.py:23
  148.2 8.3 %collective-permute-start.7 = (f32[3,2,256]{2,1,0:T(2,128)S(1)}, f32[3,2,256]{2,1,0:T(2,128)S(1)}, u32[]{:S(2)}, u32[]{:S(2)}) collective-permute-start(f32[3,2,256]{2,1,0:T(2,128)S(1)} %get-tuple-element.36), channel_id=1, source_target_pairs={{8,0},{16,8},{24,16},{32,24},{40,32},{48,40},{56,48},{64,56},{72,6... | collective-permute-start | bytes 18440 | tf_op jit(solution)/shard_map/ppermute | solution.py:24
  156.6 4.3 %collective-permute-start.8 = (f32[3,68,2]{2,1,0:T(8,128)S(1)}, f32[3,68,2]{2,1,0:T(8,128)S(1)}, u32[]{:S(2)}, u32[]{:S(2)}) collective-permute-start(f32[3,68,2]{2,1,0:T(8,128)S(1)} %get-tuple-element.31), channel_id=1, source_target_pairs={{0,1},{1,2},{2,3},{3,4},{4,5},{5,6},{6,7},{8,9},{9,10},{10,11},{11... | collective-permute-start | bytes 4904 | tf_op jit(solution)/shard_map/ppermute | solution.py:23
  158.7 5.5 %collective-permute-start.9 = (f32[3,68,2]{2,1,0:T(8,128)S(1)}, f32[3,68,2]{2,1,0:T(8,128)S(1)}, u32[]{:S(2)}, u32[]{:S(2)}) collective-permute-start(f32[3,68,2]{2,1,0:T(8,128)S(1)} %get-tuple-element.32), channel_id=1, source_target_pairs={{1,0},{2,1},{3,2},{4,3},{5,4},{6,5},{7,6},{9,8},{10,9},{11,10},{12... | collective-permute-start | bytes 4904 | tf_op jit(solution)/shard_map/ppermute | solution.py:24
  (15 other events, 37.3 us)
where the time goes:
time: 167 us; the launch traced here: 166 us
  starting transfers between devices  49.6 us (30%)
  matrix products  37.1 us (22%)
  local copies, waits for them, and re-layouts  31.6 us (19%)
  waiting for transfers between devices  28.4 us (17%)
  other arithmetic  17.8 us (11%)
    ppermute x5, starting transfers between devices, padded_2(): before = lax.ppermute(last, axis, up)  20.9 us
    ppermute x5, waiting for transfers between devices, padded_2(): after = lax.ppermute(first, axis, down)  19.6 us
    scatter-add x1, other arithmetic, face_terms(): return empty_sum.at[:, :, element].add(lifted)  10.5 us
    dot_general x2, matrix products, project_faces(): jnp.einsum('nbm,bqm->nqm', chosen_proj, picked, precision=EXACT_PRECISION)  10.4 us
    dot_general x15, matrix products, derivative(): jnp.einsum('cpe,pq->cqe', basis_mixed, jacobians[direction], precision=EX...  9.31 us
    dot_general x15, matrix products, derivative(): jnp.einsum('cb,bqe->cqe', stiffness[direction], field_in, precision=EXACT...  8.74 us
    concatenate x6, local copies, waits for them, and re-layouts, body(): jnp.concatenate([got_peer.reshape(trace_width, peer_total), edge_rim[:, 0...  8.69 us
    ppermute x5, starting transfers between devices, padded_2(): after = lax.ppermute(first, axis, down)  8.35 us
  transfers between devices with their start and end apart: 13, of which 6 were waited for; matrix products, arithmetic and copies ran while one was open for 33% of the time, Pallas kernels for 0%

commit v1 on v0

v1 whole, which is shorter than its diff:
```python
import functools

import jax
import jax.numpy as jnp
from jax import lax
from jax.experimental import pallas as pl
from jax.experimental.pallas import tpu as pltpu
from jax.sharding import PartitionSpec as P

ORDER = 5
CAP = 16
EARTH_STEP = 0.5
COURANT = 0.45
MESH = pl.DeviceIdType.MESH
F32, BF16, I32 = jnp.float32, jnp.bfloat16, jnp.int32
LANES = 128
FACE_ROWS = 24
INFO = 224
RIM = 4
DIRECTIONS = ((1, 0), (-1, 0), (0, 1), (0, -1), (1, 1), (1, -1), (-1, 1), (-1, -1))
WAY = {d: i for i, d in enumerate(DIRECTIONS)}


def split(x):
    high = x.astype(BF16)
    return high, (x - high.astype(F32)).astype(BF16)


def mm(a, b, left=1, right=0):
    return lax.dot_general(a, b, (((left,), (right,)), ((), ())), preferred_element_type=F32)


def iota(shape, axis):
    return lax.broadcasted_iota(I32, shape, axis)


def repeat_rows(rows, count):
    return jnp.concatenate(
        [jnp.broadcast_to(rows[i : i + 1], (count, rows.shape[1])) for i in range(rows.shape[0])], 0
    )


def as_column(rows, first=0):
    count = rows.shape[1] if first == 0 else CAP
    wide = repeat_rows(rows, count)
    mine = (iota(wide.shape, 0) & (count - 1)) == iota(wide.shape, 1) - first
    return jnp.sum(jnp.where(mine, wide, 0.0), axis=1, keepdims=True)


def pack_edge(array, last, base):
    lane = iota((8, LANES), 1)
    start = array.shape[1] - LANES if last else 0
    keep = lane >= LANES - RIM if last else lane < RIM
    packed = jnp.zeros((8, LANES), F32)
    for g in range(array.shape[0] // 8):
        tile = jnp.where(keep, array[8 * g : 8 * g + 8, start : start + LANES], 0.0)
        packed = packed + pltpu.roll(tile, (RIM * (g + 1 if last else g) + base) % LANES, 1)
    return packed


def extend(array, low, high, left, right, corners, base):
    lane, row = iota((8, LANES), 1), iota((8, LANES), 0)
    side = jnp.concatenate(
        [
            jnp.where(
                lane < LANES // 2,
                pltpu.roll(right, (-RIM * g - base) % LANES, 1),
                pltpu.roll(left, (LANES - RIM - RIM * g - base) % LANES, 1),
            )
            for g in range(array.shape[0] // 8)
        ],
        0,
    )
    down_right, down_left, up_right, up_left = corners
    corner = jnp.where(
        row < RIM,
        jnp.where(lane < LANES // 2, down_right, down_left),
        jnp.where(lane < LANES // 2, up_right, up_left),
    )
    bottom = jnp.where(iota(low.shape, 0) < RIM, high, low)
    return jnp.concatenate(
        [jnp.concatenate([array, side], 1), jnp.concatenate([bottom, corner], 1)], 0
    )


def shifted(array, axis):
    size = array.shape[axis]
    return (pltpu.roll(array, size - 1, axis) - pltpu.roll(array, 1, axis)) * 0.5


def kernel(mesh_count, sub_count, *refs):
    (
        state_in, scales_in, stiff_in, jac_in, proj_in, lift_in, flux_in,
        psend_in, precv_in, esend_in, erecv_in, uplift_in,
        felem_in, fdest_in, frow_in, fslip_in, sea_in, vel_in, depth_in,
        new_out, sea_out, flow_out,
        state, scales, stiff, jac, proj, lift, flux,
        psend, precv, esend, erecv, uplift,
        felem, fdest, frow, fslip, sea, vel, depth,
        matrix, matrix_hi, matrix_lo, faces, lifts, traces_out, traces_in, items_out, items_in,
        rows_out, cols_out, rows_in, cols_in, corner_in,
        height, hcols_out, hrows_in, hcols_in, hcorner_in, new, sea_buf, flow_buf,
        load_sem, store_sem, rim_send, rim_recv, trace_send, trace_recv,
        item_send, item_recv, high_send, high_recv,
    ) = refs
    quantities, basis = flux.shape[0], stiff.shape[1]
    width = quantities * basis
    padded = matrix.shape[0]
    elements = state.shape[1]
    slots = psend.shape[1]
    edge_slots = esend.shape[1]
    peer_total = sub_count * slots
    send_total = peer_total + 2 * edge_slots
    me, sub = lax.axis_index("mesh"), lax.axis_index("sub")

    def device(dm, ds):
        return (lax.rem(me + dm + mesh_count, mesh_count), lax.rem(sub + ds + sub_count, sub_count))

    loads = [
        pltpu.make_async_copy(src, dst, load_sem.at[i])
        for i, (src, dst) in enumerate(
            (
                (stiff_in, stiff), (jac_in, jac), (state_in, state), (scales_in, scales),
                (vel_in, vel), (depth_in, depth), (proj_in, proj), (flux_in, flux),
                (psend_in, psend), (precv_in, precv), (esend_in, esend), (erecv_in, erecv),
                (felem_in, felem), (fdest_in, fdest), (frow_in, frow), (fslip_in, fslip),
                (uplift_in, uplift), (lift_in, lift), (sea_in, sea),
            )
        )
    ]
    for load in loads:
        load.start()
    barrier = pltpu.get_barrier_semaphore()
    partners = [(0, k) for k in range(1, sub_count)] + [d for d in DIRECTIONS if d[0] != 0]
    for dm, ds in partners:
        pl.semaphore_signal(barrier, inc=1, device_id=device(dm, ds), device_id_type=MESH)

    def send(src, dst, send_sem, recv_sem, dm, ds):
        copy = pltpu.make_async_remote_copy(
            src_ref=src, dst_ref=dst, send_sem=send_sem, recv_sem=recv_sem,
            device_id=device(dm, ds), device_id_type=MESH,
        )
        copy.start()
        return copy

    lane = iota((1, padded), 1)
    of_quantity = sum((lane >= basis * k).astype(I32) for k in range(1, quantities + 1))
    of_basis = lane - basis * of_quantity
    spread_basis = (iota((basis, padded), 0) == of_basis).astype(F32).astype(BF16)
    spread_quantity = (iota((quantities, padded), 0) == of_quantity).astype(F32)
    loads[0].wait()
    loads[1].wait()
    stiff_hi, stiff_lo = split(stiff[...])
    stiff_wide = mm(stiff_hi, spread_basis) + mm(stiff_lo, spread_basis)
    jac_wide = [
        lax.dot_general(
            jac[:, d, :], spread_quantity, (((0,), (0,)), ((), ())),
            precision=lax.Precision.HIGHEST, preferred_element_type=F32,
        )
        for d in range(3)
    ]
    for q in range(quantities):
        block = stiff_wide[0:basis] * jac_wide[0][q : q + 1]
        for d in (1, 2):
            block = block + stiff_wide[d * basis : (d + 1) * basis] * jac_wide[d][q : q + 1]
        matrix[q * basis : (q + 1) * basis, :] = block
    matrix[width:, :] = jnp.zeros((padded - width, padded), F32)
    high, low = split(matrix[...])
    matrix_hi[...] = high
    matrix_lo[...] = low

    loads[4].wait()
    loads[5].wait()
    tile_rows, tile_cols = depth.shape
    for i, first in enumerate((tile_rows - 8, 0)):
        rows_out[i, 0:2] = vel[:, first : first + 8, :]
        rows_out[i, 2] = depth[first : first + 8, :]
    fields = (vel[0], vel[1], depth[...])
    group = RIM * (tile_rows // 8)
    for i, last in enumerate((True, False)):
        packed = pack_edge(fields[0], last, 0)
        for k in (1, 2):
            packed = packed + pack_edge(fields[k], last, k * group)
        cols_out[i] = packed
    pl.semaphore_wait(barrier, len(partners))

    def corner_of(ds):
        return slice(tile_cols - LANES, tile_cols) if ds > 0 else slice(0, LANES)

    rim_copies = []
    for i, (dm, ds) in enumerate(DIRECTIONS):
        if ds == 0:
            src, dst = rows_out.at[i], rows_in.at[i]
        elif dm == 0:
            src, dst = cols_out.at[i - 2], cols_in.at[i - 2]
        else:
            src = rows_out.at[0 if dm > 0 else 1, :, :, corner_of(ds)]
            dst = corner_in.at[i - 4]
        rim_copies.append(send(src, dst, rim_send.at[i], rim_recv.at[i], dm, ds))

    loads[2].wait()
    loads[3].wait()
    scale = scales[...]

    def derivative(x):
        x_hi, x_lo = split(x)
        both = mm(matrix_hi[...], jnp.concatenate([x_hi, x_lo], 1))
        return (both[:, :elements] + both[:, elements:] + mm(matrix_lo[...], x_hi)) * scale

    start = jnp.concatenate([state[...], jnp.zeros((padded - width, elements), F32)], 0)
    factor = EARTH_STEP
    integral = factor * start
    current = start
    for power in range(1, ORDER):
        current = derivative(current)
        factor = factor * EARTH_STEP / (power + 1)
        integral = integral + factor * current

    for i in (6, 7, 8, 9, 10, 11):
        loads[i].wait()
    codes = jnp.concatenate(
        [as_column(ref[...].astype(F32)) for ref in (psend, esend, precv, erecv)], 0
    )
    face_lane = iota((1, 4 * elements), 1)
    key = (4 * (face_lane & (elements - 1)) + face_lane // elements).astype(F32)
    hot = (codes == key).astype(F32).astype(BF16)

    faces[...] = jnp.zeros(faces.shape, F32)
    for f in range(4):
        faces[f * FACE_ROWS : f * FACE_ROWS + proj.shape[0], :] = proj[:, f, :]
    faces_hi, faces_lo = split(faces[...])
    parts = [integral[p * basis : (p + 1) * basis] for p in range(quantities)]
    mixed = []
    for q in range(quantities):
        total = flux[0, q] * parts[0]
        for p in range(1, quantities):
            total = total + flux[p, q] * parts[p]
        mixed.append(total)
    mixed_hi, mixed_lo = split(jnp.concatenate(mixed, 1))
    every = mm(faces_hi, mixed_hi) + mm(faces_hi, mixed_lo) + mm(faces_lo, mixed_hi)
    face_width = quantities * FACE_ROWS
    trace_rows = traces_out.shape[1]

    def face_block(f, q):
        return every[f * FACE_ROWS : (f + 1) * FACE_ROWS, q * elements : (q + 1) * elements]

    table = jnp.concatenate(
        [jnp.concatenate([face_block(f, q) for q in range(quantities)], 0) for f in range(4)], 1
    )
    table = jnp.concatenate([table, jnp.zeros((trace_rows - face_width, 4 * elements), F32)], 0)
    table_hi, table_lo = split(table)
    picked = mm(hot, table_hi, 1, 1) + mm(hot, table_lo, 1, 1)

    for i in (12, 13, 14, 15):
        loads[i].wait()
    fault_count = fdest.shape[1]
    square = (fault_count, fault_count)
    dest_row = fdest[...].astype(F32)
    dest_col = as_column(dest_row)
    same = dest_col == dest_row
    rank_row = jnp.sum(
        jnp.where(same & (iota(square, 0) < iota(square, 1)), 1.0, 0.0), axis=0, keepdims=True
    )
    rank_col = jnp.sum(
        jnp.where(same & (iota(square, 1) < iota(square, 0)), 1.0, 0.0), axis=1, keepdims=True
    )
    row_numbers = frow[...].astype(F32) + 1.0
    info_left = jnp.where(
        dest_row == (iota((peer_total, fault_count), 0) // slots).astype(F32), row_numbers, 0.0
    )
    info_lane = INFO % LANES
    info_right = (
        rank_col == (iota((fault_count, LANES), 1) - info_lane).astype(F32)
    ).astype(F32)
    info = mm(info_left.astype(BF16), info_right.astype(BF16)) - 1.0
    info_lanes = iota((peer_total, LANES), 1)
    info_here = (info_lanes >= info_lane) & (info_lanes < info_lane + CAP)

    traces_out[:, 0:LANES] = picked[0:send_total, 0:LANES]
    traces_out[0:peer_total, LANES:] = jnp.where(
        info_here, info, picked[0:peer_total, LANES:]
    )
    traces_out[peer_total:, LANES:] = picked[peer_total:send_total, LANES:]
    own_trace = picked[send_total:]

    def peer_block(index, rows):
        return pl.ds(pl.multiple_of(index * rows, rows), rows)

    order = sorted(range(1, sub_count), key=lambda k: -min(k, sub_count - k))
    trace_copies = []
    for k in order:
        _, peer = device(0, k)
        trace_copies.append(
            send(
                traces_out.at[peer_block(peer, slots), :], traces_in.at[peer_block(sub, slots), :],
                trace_send.at[k], trace_recv.at[k], 0, k,
            )
        )
    for i, dm in enumerate((1, -1)):
        source = peer_total + (edge_slots if dm > 0 else 0)
        target = peer_total + (0 if dm > 0 else edge_slots)
        trace_copies.append(
            send(
                traces_out.at[source : source + edge_slots, :],
                traces_in.at[target : target + edge_slots, :],
                trace_send.at[sub_count + i], trace_recv.at[sub_count + i], dm, 0,
            )
        )
    own_block = pltpu.make_async_copy(
        traces_out.at[peer_block(sub, slots), :], traces_in.at[peer_block(sub, slots), :],
        trace_recv.at[0],
    )
    own_block.start()

    base = start + derivative(integral)
    loads[17].wait()
    lifts[...] = jnp.zeros(lifts.shape, F32)
    for f in range(4):
        lifts[f * FACE_ROWS : f * FACE_ROWS + lift.shape[0], :] = lift[:, f, :]
    lift_hi, lift_lo = split(jnp.transpose(lifts[...]))
    hot_in = hot[send_total:]

    loads[16].wait()
    rows_here = iota((padded, 1), 0)
    row_quantity = sum((rows_here >= basis * k).astype(I32) for k in range(1, quantities + 1))
    wanted = (rows_here - basis * row_quantity) * quantities + row_quantity
    wanted = jnp.where(rows_here < width, wanted, -1)
    permute = (iota((padded, width), 1) == wanted).astype(F32).astype(BF16)
    uplift_hi, uplift_lo = split(uplift[...])
    uplift_hi = mm(permute, uplift_hi).astype(BF16)
    uplift_lo = mm(permute, uplift_lo).astype(BF16)

    item_slots = sub_count * CAP
    place = (
        iota((item_slots, fault_count), 0).astype(F32) == dest_row * float(CAP) + rank_row
    ).astype(F32)
    elem_col = as_column(felem[...].astype(F32))
    elem_hot = (elem_col == iota((fault_count, elements), 1).astype(F32)).astype(F32)
    choose = mm(place.astype(BF16), elem_hot.astype(BF16)).astype(BF16)
    weighting = 0.3 + 0.7 * fslip[...].astype(F32)
    weight_col = jnp.sum(place * weighting, axis=1, keepdims=True)

    for copy in rim_copies:
        copy.wait_recv()

    def corners_of(ref, k=None):
        return [
            ref[WAY[way] - 4] if k is None else ref[WAY[way] - 4, k]
            for way in ((-1, -1), (-1, 1), (1, -1), (1, 1))
        ]

    extended = [
        extend(
            fields[k], rows_in[WAY[(1, 0)], k], rows_in[WAY[(-1, 0)], k],
            cols_in[0], cols_in[1], corners_of(corner_in, k), k * group,
        )
        for k in range(3)
    ]
    shape = extended[0].shape
    ext_row, ext_lane = iota(shape, 0), iota(shape, 1)
    inside = (
        ((ext_row < tile_rows) | (ext_row >= tile_rows + RIM) | (me < mesh_count - 1))
        & ((ext_row < tile_rows + RIM) | (me > 0))
        & ((ext_lane < tile_cols) | (ext_lane >= tile_cols + LANES // 2) | (sub < sub_count - 1))
        & ((ext_lane < tile_cols + LANES // 2) | (sub > 0))
    )
    flow = [extended[0], extended[1]]
    deep = jnp.where(inside, extended[2], 0.0)
    change = COURANT * (shifted(deep * flow[0], 0) + shifted(deep * flow[1], 1))

    own_block.wait()
    for copy in trace_copies:
        copy.wait_recv()
    difference = traces_in[...] - own_trace
    diff_hi, diff_lo = split(jnp.transpose(difference))
    scattered = mm(diff_hi, hot_in) + mm(diff_lo, hot_in)
    gathered = jnp.concatenate(
        [
            jnp.concatenate(
                [
                    scattered[q * FACE_ROWS : (q + 1) * FACE_ROWS, f * elements : (f + 1) * elements]
                    for f in range(4)
                ],
                0,
            )
            for q in range(quantities)
        ],
        1,
    )
    gathered_hi, gathered_lo = split(gathered)
    lifted = mm(lift_hi, gathered_hi) + mm(lift_hi, gathered_lo) + mm(lift_lo, gathered_hi)
    face_sum = jnp.concatenate(
        [lifted[:, q * elements : (q + 1) * elements] for q in range(quantities)]
        + [jnp.zeros((padded - width, elements), F32)],
        0,
    )
    new_state = base + face_sum
    new[...] = new_state[0:width]
    new_copy = pltpu.make_async_copy(new, new_out, store_sem.at[0])
    new_copy.start()

    new_hi, new_lo = split(new_state)
    columns = mm(choose, new_hi, 1, 1) + mm(choose, new_lo, 1, 1)
    columns_hi, columns_lo = split(columns)
    items = mm(columns_hi, uplift_hi) + mm(columns_lo, uplift_hi) + mm(columns_hi, uplift_lo)
    items_out[...] = items * weight_col
    item_copies = []
    for k in order:
        _, peer = device(0, k)
        item_copies.append(
            send(
                items_out.at[peer_block(peer, CAP), :], items_in.at[peer_block(sub, CAP), :],
                item_send.at[k], item_recv.at[k], 0, k,
            )
        )
    own_items = pltpu.make_async_copy(
        items_out.at[peer_block(sub, CAP), :], items_in.at[peer_block(sub, CAP), :], item_recv.at[0]
    )
    own_items.start()

    got_info = traces_in[0:peer_total, LANES:]
    first_rows = jnp.concatenate([got_info[s * slots : s * slots + 1] for s in range(sub_count)], 0)
    landing_col = as_column(first_rows, info_lane)
    landing = (landing_col == iota((item_slots, LANES), 1).astype(F32)).astype(F32)
    landing = jnp.transpose(landing)[0:tile_rows].astype(BF16)
    loads[18].wait()

    own_items.wait()
    for copy in item_copies:
        copy.wait_recv()
    got_hi, got_lo = split(items_in[...])
    deposit = mm(landing, got_hi) + mm(landing, got_lo)
    level = sea[...] + deposit
    height[...] = level

    hcols_out[0] = pack_edge(level, True, 0)
    hcols_out[1] = pack_edge(level, False, 0)
    high_copies = []
    for i, (dm, ds) in enumerate(DIRECTIONS):
        rows = slice(tile_rows - 8, tile_rows) if dm > 0 else slice(0, 8)
        if ds == 0:
            src, dst = height.at[rows, :], hrows_in.at[i]
        elif dm == 0:
            src, dst = hcols_out.at[i - 2], hcols_in.at[i - 2]
        else:
            src, dst = height.at[rows, corner_of(ds)], hcorner_in.at[i - 4]
        high_copies.append(send(src, dst, high_send.at[i], high_recv.at[i], dm, ds))
    for copy in high_copies:
        copy.wait_recv()
    level = extend(
        level, hrows_in[WAY[(1, 0)]], hrows_in[WAY[(-1, 0)]], hcols_in[0], hcols_in[1],
        corners_of(hcorner_in), 0,
    )
    level = jnp.where(inside, level, 0.0) - change
    flow = [flow[axis] - COURANT * shifted(level, axis) for axis in (0, 1)]
    level = jnp.where(inside, level, 0.0)
    level = level - COURANT * (shifted(deep * flow[0], 0) + shifted(deep * flow[1], 1))
    flow = [flow[axis] - COURANT * shifted(level, axis) for axis in (0, 1)]
    sea_buf[...] = level[0:tile_rows, 0:tile_cols]
    flow_buf[0] = flow[0][0:tile_rows, 0:tile_cols]
    flow_buf[1] = flow[1][0:tile_rows, 0:tile_cols]
    sea_copy = pltpu.make_async_copy(sea_buf, sea_out, store_sem.at[1])
    flow_copy = pltpu.make_async_copy(flow_buf, flow_out, store_sem.at[2])
    sea_copy.start()
    flow_copy.start()
    for copy in rim_copies + trace_copies + item_copies + high_copies:
        copy.wait_send()
    new_copy.wait()
    sea_copy.wait()
    flow_copy.wait()


def body(mesh_count, sub_count, *arguments):
    (
        state, scales, stiffness, jacobians, projection, lifting, flux_matrix,
        peer_send, peer_recv, edge_send, edge_recv, uplift_map,
        fault_elem, fault_dest, fault_row, fault_slip, sea_level, velocity, depth,
    ) = arguments
    basis, quantities, elements = state.shape
    width = basis * quantities
    faults = fault_elem.shape[0]
    rows, cols = sea_level.shape
    slots, edge_slots = peer_send.shape[2], edge_send.shape[2]
    operands = (
        jnp.transpose(state, (1, 0, 2)).reshape(width, elements),
        scales.reshape(1, elements),
        stiffness.reshape(3 * basis, basis),
        jnp.transpose(jacobians, (1, 0, 2)),
        jnp.transpose(projection, (1, 0, 2)),
        jnp.transpose(lifting, (2, 0, 1)),
        flux_matrix,
        peer_send.reshape(sub_count, slots),
        peer_recv.reshape(sub_count, slots),
        edge_send.reshape(2, edge_slots),
        edge_recv.reshape(2, edge_slots),
        uplift_map,
        fault_elem.reshape(1, faults),
        fault_dest.reshape(1, faults),
        fault_row.reshape(1, faults),
        fault_slip.reshape(1, faults),
        sea_level,
        velocity,
        depth,
    )
    padded = -(-width // LANES) * LANES
    trace_lanes = 2 * LANES
    send_total = sub_count * slots + 2 * edge_slots
    item_slots = sub_count * CAP
    vmem, dma = pltpu.VMEM, pltpu.SemaphoreType.DMA
    held = [
        (pltpu.SMEM if i == 6 else vmem)(x.shape, x.dtype) for i, x in enumerate(operands)
    ]
    scratch = held + [
        vmem((padded, padded), F32),
        vmem((padded, padded), BF16),
        vmem((padded, padded), BF16),
        vmem((4 * FACE_ROWS, basis), F32),
        vmem((4 * FACE_ROWS, basis), F32),
        vmem((send_total, trace_lanes), F32),
        vmem((send_total, trace_lanes), F32),
        vmem((item_slots, cols), F32),
        vmem((item_slots, cols), F32),
        vmem((2, 3, 8, cols), F32),
        vmem((2, 8, LANES), F32),
        vmem((2, 3, 8, cols), F32),
        vmem((2, 8, LANES), F32),
        vmem((4, 3, 8, LANES), F32),
        vmem((rows, cols), F32),
        vmem((2, 8, LANES), F32),
        vmem((2, 8, cols), F32),
        vmem((2, 8, LANES), F32),
        vmem((4, 8, LANES), F32),
        vmem((width, elements), F32),
        vmem((rows, cols), F32),
        vmem((2, rows, cols), F32),
        dma((len(operands),)),
        dma((3,)),
        dma((8,)),
        dma((8,)),
        dma((sub_count + 2,)),
        dma((sub_count + 2,)),
        dma((sub_count,)),
        dma((sub_count,)),
        dma((8,)),
        dma((8,)),
    ]
    hbm = pl.BlockSpec(memory_space=pltpu.HBM)
    new_state, sea_out, flow_out = pl.pallas_call(
        functools.partial(kernel, mesh_count, sub_count),
        out_shape=(
            jax.ShapeDtypeStruct((width, elements), F32),
            jax.ShapeDtypeStruct((rows, cols), F32),
            jax.ShapeDtypeStruct((2, rows, cols), F32),
        ),
        in_specs=[hbm] * len(operands),
        out_specs=(hbm, hbm, hbm),
        scratch_shapes=scratch,
        compiler_params=pltpu.CompilerParams(
            collective_id=0, has_side_effects=True, vmem_limit_bytes=63 * 1024 * 1024
        ),
    )(*operands)
    new_state = jnp.transpose(new_state.reshape(quantities, basis, elements), (1, 0, 2))
    return new_state, sea_out, flow_out


def solution(mesh):
    device = P(("mesh", "sub"))
    return jax.shard_map(
        functools.partial(body, mesh.shape["mesh"], mesh.shape["sub"]),
        mesh=mesh,
        in_specs=(
            P(None, None, ("mesh", "sub")),
            device,
            P(),
            P(),
            P(),
            P(),
            P(),
            P(("mesh", "sub"), None, None),
            P(("mesh", "sub"), None, None),
            P(("mesh", "sub"), None, None),
            P(("mesh", "sub"), None, None),
            P(),
            device,
            P(("mesh", "sub"), None),
            device,
            device,
            P("mesh", "sub"),
            P(None, "mesh", "sub"),
            P("mesh", "sub"),
        ),
        out_specs=(P(None, None, ("mesh", "sub")), P("mesh", "sub"), P(None, "mesh", "sub")),
        check_vma=False,
    )
```

time: 167 us -> 42.5 us (0.25)
  the two profiles are of different devices: /device:TPU:199 before, /device:TPU:1 now
where the time goes in v1:
time: 42.5 us; the launch traced here: 42.3 us
  Pallas kernels  38.4 us (90%)
  local copies, waits for them, and re-layouts  3.28 us (8%)
  between operations  0.66 us (2%)
    pallas_call x1, Pallas kernels, body(): pl.pallas_call(functools.partial(kernel, mesh_count, sub_count), out_shap...  38.4 us
    unnamed x7, local copies, waits for them, and re-layouts  3.28 us

profile of v1, /device:TPU:1, one launch (start us, length us, event | category | flops | bytes accessed | tf_op | source)
XLA Modules:
  0.0 42.3 jit_solution(13068565813806481980)
XLA Ops:
  0.6 38.4 %shard_map.202 = (f32[504,128]{1,0:T(8,128)}, f32[64,256]{1,0:T(8,128)}, f32[2,64,256]{2,1,0:T(8,128)}) custom-call(f32[504,128]{1,0:T(8,128)} %bitcast.20, f32[1,128]{1,0:T(1,128)} %bitcast.29, f32[168,56]{1,0:T(8,128)} %bitcast.21, f32[9,3,9]{2,1,0:T(4,128)} %bitcast.24, f32[21,4,56]{2,1,0:T(4,128)} %bitcast.22, f32[21,4,56]{2,1,0:T(4,128)} %bitcast.23, ...), custom_call_target="tpu_custom_call" | custom-call | tf_op jit(solution)/shard_map/pallas_call | solution.py:548
  39.0 0.0 copy-start.1
  39.0 1.7 %copy.25 = f32[56,9,128]{2,0,1:T(8,128)} copy(f32[56,9,128]{2,0,1:T(8,128)} %bitcast.19) | data formatting | bytes 516096
  40.7 0.0 copy-done.1
  40.7 0.0 copy-start
  40.7 0.6 %copy.26 = f32[64,256]{1,0:T(8,128)} copy(f32[64,256]{1,0:T(8,128)S(1)} %copy-done.1) | data formatting | bytes 131072
  41.4 0.3 copy-done
  41.7 0.7 %copy.27 = f32[2,64,256]{2,1,0:T(8,128)} copy(f32[2,64,256]{2,1,0:T(8,128)S(1)} %copy-done) | data formatting | bytes 262144
Async XLA Ops:
  39.0 1.7 %copy-start.1 = (f32[64,256]{1,0:T(8,128)S(1)}, f32[64,256]{1,0:T(8,128)}, u32[]{:S(2)}) copy-start(f32[64,256]{1,0:T(8,128)} %get-tuple-element.13) | copy-start | bytes 196612
  40.7 0.9 %copy-start = (f32[2,64,256]{2,1,0:T(8,128)S(1)}, f32[2,64,256]{2,1,0:T(8,128)}, u32[]{:S(2)}) copy-start(f32[2,64,256]{2,1,0:T(8,128)} %get-tuple-element.14) | copy-start | bytes 393220

commit v2 on v1

v2 whole, which is shorter than its diff:
```python
import functools

import jax
import jax.numpy as jnp
from jax import lax
from jax.experimental import pallas as pl
from jax.experimental.pallas import tpu as pltpu
from jax.sharding import PartitionSpec as P

ORDER = 5
CAP = 16
EARTH_STEP = 0.5
COURANT = 0.45
MESH = pl.DeviceIdType.MESH
F32, BF16, I32 = jnp.float32, jnp.bfloat16, jnp.int32
LANES = 128
FACE_ROWS = 24
INFO = 224
RIM = 4
DIRECTIONS = ((1, 0), (-1, 0), (0, 1), (0, -1), (1, 1), (1, -1), (-1, 1), (-1, -1))
WAY = {d: i for i, d in enumerate(DIRECTIONS)}


def split(x):
    high = x.astype(BF16)
    return high, (x - high.astype(F32)).astype(BF16)


def mm(a, b, left=1, right=0):
    return lax.dot_general(a, b, (((left,), (right,)), ((), ())), preferred_element_type=F32)


def iota(shape, axis):
    return lax.broadcasted_iota(I32, shape, axis)


def repeat_rows(rows, count):
    return jnp.concatenate(
        [jnp.broadcast_to(rows[i : i + 1], (count, rows.shape[1])) for i in range(rows.shape[0])], 0
    )


def as_column(rows, first=0):
    count = rows.shape[1] if first == 0 else CAP
    wide = repeat_rows(rows, count)
    mine = (iota(wide.shape, 0) & (count - 1)) == iota(wide.shape, 1) - first
    return jnp.sum(jnp.where(mine, wide, 0.0), axis=1, keepdims=True)


def pack_edge(array, last, base):
    lane = iota((8, LANES), 1)
    start = array.shape[1] - LANES if last else 0
    keep = lane >= LANES - RIM if last else lane < RIM
    packed = jnp.zeros((8, LANES), F32)
    for g in range(array.shape[0] // 8):
        tile = jnp.where(keep, array[8 * g : 8 * g + 8, start : start + LANES], 0.0)
        packed = packed + pltpu.roll(tile, (RIM * (g + 1 if last else g) + base) % LANES, 1)
    return packed


def extend(array, low, high, left, right, corners, base):
    lane, row = iota((8, LANES), 1), iota((8, LANES), 0)
    side = jnp.concatenate(
        [
            jnp.where(
                lane < LANES // 2,
                pltpu.roll(right, (-RIM * g - base) % LANES, 1),
                pltpu.roll(left, (LANES - RIM - RIM * g - base) % LANES, 1),
            )
            for g in range(array.shape[0] // 8)
        ],
        0,
    )
    down_right, down_left, up_right, up_left = corners
    corner = jnp.where(
        row < RIM,
        jnp.where(lane < LANES // 2, down_right, down_left),
        jnp.where(lane < LANES // 2, up_right, up_left),
    )
    bottom = jnp.where(iota(low.shape, 0) < RIM, high, low)
    return jnp.concatenate(
        [jnp.concatenate([array, side], 1), jnp.concatenate([bottom, corner], 1)], 0
    )


def shifted(array, axis):
    size = array.shape[axis]
    return (pltpu.roll(array, size - 1, axis) - pltpu.roll(array, 1, axis)) * 0.5


def kernel(mesh_count, sub_count, *refs):
    (
        state_in, scales_in, stiff_in, jac_in, proj_in, lift_in, flux_in,
        psend_in, precv_in, esend_in, erecv_in, uplift_in,
        felem_in, fdest_in, frow_in, fslip_in, sea_in, vel_in, depth_in,
        new_out, sea_out, flow_out,
        state, scales, stiff, jac, proj, lift, flux,
        psend, precv, esend, erecv, uplift,
        felem, fdest, frow, fslip, sea, vel, depth,
        spread, matrix_hi, matrix_lo, hot, faces, lifts, traces_out, traces_in, items_out, items_in,
        rows_out, cols_out, rows_in, cols_in, corner_in,
        height, hcols_out, hrows_in, hcols_in, hcorner_in,
        load_sem, rim_send, rim_recv, trace_send, trace_recv,
        item_send, item_recv, high_send, high_recv,
    ) = refs
    quantities, basis = flux.shape[0], stiff.shape[1]
    width = quantities * basis
    padded = matrix_hi.shape[0]
    elements = state.shape[1]
    slots = psend.shape[1]
    edge_slots = esend.shape[1]
    peer_total = sub_count * slots
    send_total = peer_total + 2 * edge_slots
    tile_rows, tile_cols = depth.shape
    me, sub = lax.axis_index("mesh"), lax.axis_index("sub")
    neighbour = {1: me < mesh_count - 1, -1: me > 0}

    def device(dm, ds):
        return (me + dm, lax.rem(sub + ds + sub_count, sub_count))

    loads = [
        pltpu.make_async_copy(src, dst, load_sem.at[i])
        for i, (src, dst) in enumerate(
            (
                (stiff_in, stiff), (jac_in, jac), (state_in, state), (scales_in, scales),
                (psend_in, psend), (precv_in, precv), (esend_in, esend), (erecv_in, erecv),
                (proj_in, proj), (felem_in, felem), (fdest_in, fdest), (frow_in, frow),
                (fslip_in, fslip), (flux_in, flux), (lift_in, lift),
                (vel_in, vel), (depth_in, depth), (uplift_in, uplift), (sea_in, sea),
            )
        )
    ]
    for load in loads:
        load.start()
    barrier = pltpu.get_barrier_semaphore()

    def greet(dm, ds):
        pl.semaphore_signal(barrier, inc=1, device_id=device(dm, ds), device_id_type=MESH)

    for k in range(1, sub_count):
        greet(0, k)
    for side in (1, -1):

        @pl.when(neighbour[side])
        def _():
            for ds in (0, 1, -1):
                greet(side, ds)

    def remote(src, dst, send_sem, recv_sem, dm, ds):
        return pltpu.make_async_remote_copy(
            src_ref=src, dst_ref=dst, send_sem=send_sem, recv_sem=recv_sem,
            device_id=device(dm, ds), device_id_type=MESH,
        )

    def each(copies, act):
        for dm, copy in copies:
            if dm == 0:
                act(copy)
        for side in (1, -1):
            some = [copy for dm, copy in copies if dm == side]
            if some:

                @pl.when(neighbour[side])
                def _():
                    for copy in some:
                        act(copy)

    def start_all(copies):
        each(copies, lambda copy: copy.start())

    def sent_all(copies):
        each(copies, lambda copy: copy.wait_send())

    def received_all(copies):
        each([(-dm, copy) for dm, copy in copies], lambda copy: copy.wait_recv())

    def rim_copies(rows_of, cols_ref, rows_ref, cols_got, corner_ref, send_sem, recv_sem):
        copies = []
        for i, (dm, ds) in enumerate(DIRECTIONS):
            if ds == 0:
                src, dst = rows_of(dm, None), rows_ref.at[i]
            elif dm == 0:
                src, dst = cols_ref.at[i - 2], cols_got.at[i - 2]
            else:
                lanes = slice(tile_cols - LANES, tile_cols) if ds > 0 else slice(0, LANES)
                src, dst = rows_of(dm, lanes), corner_ref.at[i - 4]
            copies.append((dm, remote(src, dst, send_sem.at[i], recv_sem.at[i], dm, ds)))
        return copies

    lane = iota((1, padded), 1)
    of_quantity = sum((lane >= basis * k).astype(I32) for k in range(1, quantities + 1))
    of_basis = lane - basis * of_quantity
    spread_basis = (iota((basis, padded), 0) == of_basis).astype(F32).astype(BF16)
    spread_quantity = (iota((quantities, padded), 0) == of_quantity).astype(F32)
    for load in loads[0:15]:
        load.wait()
    stiff_hi, stiff_lo = split(stiff[...])
    spread[...] = mm(stiff_hi, spread_basis) + mm(stiff_lo, spread_basis)
    jac_wide = [
        lax.dot_general(
            jac[:, d, :], spread_quantity, (((0,), (0,)), ((), ())),
            precision=lax.Precision.HIGHEST, preferred_element_type=F32,
        )
        for d in range(3)
    ]

    def matrix_rows(q):
        if q == quantities:
            return jnp.zeros((padded - width, padded), F32)
        block = spread[0:basis, :] * jac_wide[0][q : q + 1]
        for d in (1, 2):
            block = block + spread[d * basis : (d + 1) * basis, :] * jac_wide[d][q : q + 1]
        return block

    at = 0
    for q in range(0, quantities, 2):
        high, low = split(jnp.concatenate([matrix_rows(q), matrix_rows(q + 1)], 0))
        matrix_hi[at : at + high.shape[0], :] = high
        matrix_lo[at : at + high.shape[0], :] = low
        at = at + high.shape[0]

    codes = jnp.concatenate(
        [as_column(ref[...].astype(F32)) for ref in (psend, esend, precv, erecv)], 0
    )
    face_lane = iota((1, 4 * elements), 1)
    key = (4 * (face_lane & (elements - 1)) + face_lane // elements).astype(F32)
    hot[...] = (codes == key).astype(F32).astype(BF16)
    faces[...] = jnp.zeros(faces.shape, F32)
    for f in range(4):
        for half in (0, LANES // 2):
            faces[f * FACE_ROWS : f * FACE_ROWS + proj.shape[0], half : half + basis] = proj[:, f, :]
    faces_hi, faces_lo = split(faces[...])
    faces_lo = faces_lo[:, 0 : LANES // 2]

    fault_count = fdest.shape[1]
    square = (fault_count, fault_count)
    dest_row = fdest[...].astype(F32)
    dest_col = as_column(dest_row)
    same = dest_col == dest_row
    rank_row = jnp.sum(
        jnp.where(same & (iota(square, 0) < iota(square, 1)), 1.0, 0.0), axis=0, keepdims=True
    )
    rank_col = jnp.sum(
        jnp.where(same & (iota(square, 1) < iota(square, 0)), 1.0, 0.0), axis=1, keepdims=True
    )
    row_numbers = frow[...].astype(F32) + 1.0
    info_left = jnp.where(
        dest_row == (iota((peer_total, fault_count), 0) // slots).astype(F32), row_numbers, 0.0
    )
    info_lane = INFO % LANES
    info_right = (
        rank_col == (iota((fault_count, LANES), 1) - info_lane).astype(F32)
    ).astype(F32)
    info = mm(info_left.astype(BF16), info_right.astype(BF16)) - 1.0
    info_lanes = iota((peer_total, LANES), 1)
    info_here = (info_lanes >= info_lane) & (info_lanes < info_lane + CAP)

    scale = scales[...]

    def derivative(x):
        x_hi, x_lo = split(x)
        both = mm(matrix_hi[...], jnp.concatenate([x_hi, x_lo], 1))
        return (both[:, :elements] + both[:, elements:] + mm(matrix_lo[...], x_hi)) * scale

    start = jnp.concatenate([state[...], jnp.zeros((padded - width, elements), F32)], 0)
    factor = EARTH_STEP
    integral = factor * start
    current = start
    for power in range(1, ORDER):
        current = derivative(current)
        factor = factor * EARTH_STEP / (power + 1)
        integral = integral + factor * current

    parts = jnp.concatenate(
        [
            jnp.concatenate(
                [
                    integral[p * basis : (p + 1) * basis],
                    jnp.zeros((LANES // 2 - basis, elements), F32),
                ],
                0,
            )
            for p in range(quantities)
        ],
        1,
    )
    parts_hi, parts_lo = split(parts)
    every = mm(faces_hi, jnp.concatenate([parts_hi, parts_lo], 0)) + mm(faces_lo, parts_hi)
    face_width = quantities * FACE_ROWS
    trace_rows = traces_out.shape[1]

    def face_block(f, q):
        return every[f * FACE_ROWS : (f + 1) * FACE_ROWS, q * elements : (q + 1) * elements]

    table = jnp.concatenate(
        [jnp.concatenate([face_block(f, q) for q in range(quantities)], 0) for f in range(4)], 1
    )
    table = jnp.concatenate([table, jnp.zeros((trace_rows - face_width, 4 * elements), F32)], 0)
    table_hi, table_lo = split(table)
    picked = mm(hot[...], table_hi, 1, 1) + mm(hot[...], table_lo, 1, 1)
    traces_out[:, 0:LANES] = picked[0:send_total, 0:LANES]
    traces_out[0:peer_total, LANES:] = jnp.where(
        info_here, info, picked[0:peer_total, LANES:]
    )
    traces_out[peer_total:, LANES:] = picked[peer_total:send_total, LANES:]
    own_trace = picked[send_total:]

    def peer_block(index, rows):
        return pl.ds(pl.multiple_of(index * rows, rows), rows)

    order = sorted(range(1, sub_count), key=lambda k: -min(k, sub_count - k))
    trace_copies = []
    for k in order:
        _, peer = device(0, k)
        trace_copies.append(
            (
                0,
                remote(
                    traces_out.at[peer_block(peer, slots), :],
                    traces_in.at[peer_block(sub, slots), :],
                    trace_send.at[k], trace_recv.at[k], 0, k,
                ),
            )
        )
    for i, dm in enumerate((1, -1)):
        source = peer_total + (edge_slots if dm > 0 else 0)
        target = peer_total + (0 if dm > 0 else edge_slots)
        trace_copies.append(
            (
                dm,
                remote(
                    traces_out.at[source : source + edge_slots, :],
                    traces_in.at[target : target + edge_slots, :],
                    trace_send.at[sub_count + i], trace_recv.at[sub_count + i], dm, 0,
                ),
            )
        )
    pl.semaphore_wait(
        barrier, sub_count - 1 + 3 * (neighbour[1].astype(I32) + neighbour[-1].astype(I32))
    )
    start_all(trace_copies)
    own_block = pltpu.make_async_copy(
        traces_out.at[peer_block(sub, slots), :], traces_in.at[peer_block(sub, slots), :],
        trace_recv.at[0],
    )
    own_block.start()

    for load in loads[15:]:
        load.wait()
    for i, first in enumerate((tile_rows - 8, 0)):
        rows_out[i, 0:2] = vel[:, first : first + 8, :]
        rows_out[i, 2] = depth[first : first + 8, :]
    fields = (vel[0], vel[1], depth[...])
    group = RIM * (tile_rows // 8)
    for i, last in enumerate((True, False)):
        packed = pack_edge(fields[0], last, 0)
        for k in (1, 2):
            packed = packed + pack_edge(fields[k], last, k * group)
        cols_out[i] = packed

    def rows_of_fields(dm, lanes):
        i = 0 if dm > 0 else 1
        return rows_out.at[i] if lanes is None else rows_out.at[i, :, :, lanes]

    field_copies = rim_copies(
        rows_of_fields, cols_out, rows_in, cols_in, corner_in, rim_send, rim_recv
    )
    start_all(field_copies)

    base = start + derivative(integral)
    lifts[...] = jnp.zeros(lifts.shape, F32)
    for f in range(4):
        lifts[f * FACE_ROWS : f * FACE_ROWS + lift.shape[0], :] = lift[:, f, :]
    lift_hi, lift_lo = split(jnp.transpose(lifts[...]))
    lift_hi = jnp.concatenate([lift_hi, lift_hi], 1)
    hot_in = hot[send_total:, :]
    hot_in = jnp.concatenate([hot_in, hot_in], 0)

    face_col, face_row = iota((trace_rows, 1), 0), iota((1, trace_rows), 1)
    quantity_col = sum((face_col >= FACE_ROWS * k).astype(I32) for k in range(1, quantities + 1))
    quantity_row = sum((face_row >= FACE_ROWS * k).astype(I32) for k in range(1, quantities + 1))
    exact = functools.partial(
        lax.dot_general, precision=lax.Precision.HIGHEST, preferred_element_type=F32
    )
    flux_left = exact(
        (quantity_col == iota((trace_rows, quantities), 1)).astype(F32), flux[...],
        (((1,), (1,)), ((), ())),
    )
    flux_wide = exact(
        flux_left, (quantity_row == iota((quantities, trace_rows), 0)).astype(F32),
        (((1,), (0,)), ((), ())),
    )
    same_face = face_col - FACE_ROWS * quantity_col == face_row - FACE_ROWS * quantity_row
    flux_hi, flux_lo = split(jnp.where(same_face, flux_wide, 0.0))

    rows_here = iota((padded, 1), 0)
    row_quantity = sum((rows_here >= basis * k).astype(I32) for k in range(1, quantities + 1))
    wanted = (rows_here - basis * row_quantity) * quantities + row_quantity
    wanted = jnp.where(rows_here < width, wanted, -1)
    permute = (iota((padded, width), 1) == wanted).astype(F32).astype(BF16)
    uplift_hi, uplift_lo = split(uplift[...])
    uplift_hi = mm(permute, uplift_hi).astype(BF16)
    uplift_lo = mm(permute, uplift_lo).astype(BF16)

    item_slots = sub_count * CAP
    place = (
        iota((item_slots, fault_count), 0).astype(F32) == dest_row * float(CAP) + rank_row
    ).astype(F32)
    elem_col = as_column(felem[...].astype(F32))
    elem_hot = (elem_col == iota((fault_count, elements), 1).astype(F32)).astype(F32)
    choose = mm(place.astype(BF16), elem_hot.astype(BF16)).astype(BF16)
    choose = jnp.concatenate([choose, choose], 1)
    weighting = 0.3 + 0.7 * fslip[...].astype(F32)
    weight_col = jnp.sum(place * weighting, axis=1, keepdims=True)

    own_block.wait()
    received_all(trace_copies)
    slot_col = iota((send_total, 1), 0)
    missing = ((slot_col >= peer_total) & (slot_col < peer_total + edge_slots) & (me == 0)) | (
        (slot_col >= peer_total + edge_slots) & (me == mesh_count - 1)
    )
    difference = jnp.where(missing, 0.0, traces_in[...]) - own_trace
    diff_hi, diff_lo = split(difference)
    mixed = mm(flux_hi, jnp.concatenate([diff_hi, diff_lo], 0), 1, 1)
    mixed = mixed[:, :send_total] + mixed[:, send_total:] + mm(flux_lo, diff_hi, 1, 1)
    scattered = mm(jnp.concatenate(split(mixed), 1), hot_in)
    gathered = jnp.concatenate(
        [
            jnp.concatenate(
                [
                    scattered[q * FACE_ROWS : (q + 1) * FACE_ROWS, f * elements : (f + 1) * elements]
                    for f in range(4)
                ],
                0,
            )
            for q in range(quantities)
        ],
        1,
    )
    gathered_hi, gathered_lo = split(gathered)
    lifted = mm(lift_hi, jnp.concatenate([gathered_hi, gathered_lo], 0)) + mm(lift_lo, gathered_hi)
    face_sum = jnp.concatenate(
        [lifted[:, q * elements : (q + 1) * elements] for q in range(quantities)]
        + [jnp.zeros((padded - width, elements), F32)],
        0,
    )
    new_state = base + face_sum
    new_out[...] = new_state[0:width]

    columns = mm(choose, jnp.concatenate(split(new_state), 1), 1, 1)
    columns_hi, columns_lo = split(columns)
    items = mm(columns_hi, uplift_hi) + mm(columns_lo, uplift_hi) + mm(columns_hi, uplift_lo)
    items_out[...] = items * weight_col
    item_copies = []
    for k in order:
        _, peer = device(0, k)
        item_copies.append(
            (
                0,
                remote(
                    items_out.at[peer_block(peer, CAP), :], items_in.at[peer_block(sub, CAP), :],
                    item_send.at[k], item_recv.at[k], 0, k,
                ),
            )
        )
    start_all(item_copies)
    own_items = pltpu.make_async_copy(
        items_out.at[peer_block(sub, CAP), :], items_in.at[peer_block(sub, CAP), :], item_recv.at[0]
    )
    own_items.start()

    got_info = traces_in[0:peer_total, LANES:]
    first_rows = jnp.concatenate([got_info[s * slots : s * slots + 1] for s in range(sub_count)], 0)
    landing_col = as_column(first_rows, info_lane)
    landing = (landing_col == iota((item_slots, LANES), 1).astype(F32)).astype(F32)
    landing = jnp.transpose(landing)[0:tile_rows].astype(BF16)
    landing = jnp.concatenate([landing, landing], 1)

    received_all(field_copies)

    def corners_of(ref, k=None):
        return [
            ref[WAY[way] - 4] if k is None else ref[WAY[way] - 4, k]
            for way in ((-1, -1), (-1, 1), (1, -1), (1, 1))
        ]

    extended = [
        extend(
            fields[k], rows_in[WAY[(1, 0)], k], rows_in[WAY[(-1, 0)], k],
            cols_in[0], cols_in[1], corners_of(corner_in, k), k * group,
        )
        for k in range(3)
    ]
    shape = extended[0].shape
    ext_row, ext_lane = iota(shape, 0), iota(shape, 1)
    inside = (
        ((ext_row < tile_rows) | (ext_row >= tile_rows + RIM) | neighbour[1])
        & ((ext_row < tile_rows + RIM) | neighbour[-1])
        & ((ext_lane < tile_cols) | (ext_lane >= tile_cols + LANES // 2) | (sub < sub_count - 1))
        & ((ext_lane < tile_cols + LANES // 2) | (sub > 0))
    )
    flow = [jnp.where(inside, extended[axis], 0.0) for axis in (0, 1)]
    deep = jnp.where(inside, extended[2], 0.0)
    change = COURANT * (shifted(deep * flow[0], 0) + shifted(deep * flow[1], 1))

    own_items.wait()
    received_all(item_copies)
    deposit = mm(landing, jnp.concatenate(split(items_in[...]), 0))
    level = sea[...] + deposit
    height[...] = level
    hcols_out[0] = pack_edge(level, True, 0)
    hcols_out[1] = pack_edge(level, False, 0)

    def rows_of_height(dm, lanes):
        rows = slice(tile_rows - 8, tile_rows) if dm > 0 else slice(0, 8)
        return height.at[rows, :] if lanes is None else height.at[rows, lanes]

    high_copies = rim_copies(
        rows_of_height, hcols_out, hrows_in, hcols_in, hcorner_in, high_send, high_recv
    )
    start_all(high_copies)
    for copies in (trace_copies, field_copies, item_copies):
        sent_all(copies)

    received_all(high_copies)
    level = extend(
        level, hrows_in[WAY[(1, 0)]], hrows_in[WAY[(-1, 0)]], hcols_in[0], hcols_in[1],
        corners_of(hcorner_in), 0,
    )
    level = jnp.where(inside, level, 0.0) - change
    flow = [flow[axis] - COURANT * shifted(level, axis) for axis in (0, 1)]
    level = jnp.where(inside, level, 0.0)
    level = level - COURANT * (shifted(deep * flow[0], 0) + shifted(deep * flow[1], 1))
    flow = [flow[axis] - COURANT * shifted(level, axis) for axis in (0, 1)]
    sea_out[...] = level[0:tile_rows, 0:tile_cols]
    flow_out[0] = flow[0][0:tile_rows, 0:tile_cols]
    flow_out[1] = flow[1][0:tile_rows, 0:tile_cols]
    sent_all(high_copies)


def store_kernel(new_in, sea_in, flow_in, new_out, sea_out, flow_out, sems):
    copies = [
        pltpu.make_async_copy(src, dst, sems.at[i])
        for i, (src, dst) in enumerate(
            ((new_in, new_out), (sea_in, sea_out), (flow_in, flow_out))
        )
    ]
    for copy in copies:
        copy.start()
    for copy in copies:
        copy.wait()


def body(mesh_count, sub_count, *arguments):
    (
        state, scales, stiffness, jacobians, projection, lifting, flux_matrix,
        peer_send, peer_recv, edge_send, edge_recv, uplift_map,
        fault_elem, fault_dest, fault_row, fault_slip, sea_level, velocity, depth,
    ) = arguments
    basis, quantities, elements = state.shape
    width = basis * quantities
    faults = fault_elem.shape[0]
    rows, cols = sea_level.shape
    slots, edge_slots = peer_send.shape[2], edge_send.shape[2]
    operands = (
        jnp.transpose(state, (1, 0, 2)).reshape(width, elements),
        scales.reshape(1, elements),
        stiffness.reshape(3 * basis, basis),
        jnp.transpose(jacobians, (1, 0, 2)),
        jnp.transpose(projection, (1, 0, 2)),
        jnp.transpose(lifting, (2, 0, 1)),
        flux_matrix,
        peer_send.reshape(sub_count, slots),
        peer_recv.reshape(sub_count, slots),
        edge_send.reshape(2, edge_slots),
        edge_recv.reshape(2, edge_slots),
        uplift_map,
        fault_elem.reshape(1, faults),
        fault_dest.reshape(1, faults),
        fault_row.reshape(1, faults),
        fault_slip.reshape(1, faults),
        sea_level,
        velocity,
        depth,
    )
    padded = -(-width // LANES) * LANES
    trace_lanes = 2 * LANES
    send_total = sub_count * slots + 2 * edge_slots
    item_slots = sub_count * CAP
    vmem, dma = pltpu.VMEM, pltpu.SemaphoreType.DMA
    held = [vmem(x.shape, x.dtype) for x in operands]
    scratch = held + [
        vmem((3 * basis, padded), F32),
        vmem((padded, padded), BF16),
        vmem((padded, padded), BF16),
        vmem((2 * send_total, 4 * elements), BF16),
        vmem((4 * FACE_ROWS, LANES), F32),
        vmem((4 * FACE_ROWS, basis), F32),
        vmem((send_total, trace_lanes), F32),
        vmem((send_total, trace_lanes), F32),
        vmem((item_slots, cols), F32),
        vmem((item_slots, cols), F32),
        vmem((2, 3, 8, cols), F32),
        vmem((2, 8, LANES), F32),
        vmem((2, 3, 8, cols), F32),
        vmem((2, 8, LANES), F32),
        vmem((4, 3, 8, LANES), F32),
        vmem((rows, cols), F32),
        vmem((2, 8, LANES), F32),
        vmem((2, 8, cols), F32),
        vmem((2, 8, LANES), F32),
        vmem((4, 8, LANES), F32),
        dma((len(operands),)),
        dma((8,)),
        dma((8,)),
        dma((sub_count + 2,)),
        dma((sub_count + 2,)),
        dma((sub_count,)),
        dma((sub_count,)),
        dma((8,)),
        dma((8,)),
    ]
    hbm, local = pl.BlockSpec(memory_space=pltpu.HBM), pl.BlockSpec(memory_space=pltpu.VMEM)
    shapes = ((width, elements), (rows, cols), (2, rows, cols))
    results = pl.pallas_call(
        functools.partial(kernel, mesh_count, sub_count),
        out_shape=tuple(vmem(shape, F32) for shape in shapes),
        in_specs=[hbm] * len(operands),
        out_specs=(local,) * 3,
        scratch_shapes=scratch,
        compiler_params=pltpu.CompilerParams(
            collective_id=0, has_side_effects=True, vmem_limit_bytes=40 * 1024 * 1024
        ),
    )(*[pltpu.with_memory_space_constraint(x, pltpu.HBM) for x in operands])
    new_state, sea_out, flow_out = pl.pallas_call(
        store_kernel,
        out_shape=tuple(pltpu.HBM(shape, F32) for shape in shapes),
        in_specs=[local] * 3,
        out_specs=(hbm,) * 3,
        scratch_shapes=[dma((3,))],
    )(*results)
    new_state = jnp.transpose(new_state.reshape(quantities, basis, elements), (1, 0, 2))
    return new_state, sea_out, flow_out


def solution(mesh):
    device = P(("mesh", "sub"))
    return jax.shard_map(
        functools.partial(body, mesh.shape["mesh"], mesh.shape["sub"]),
        mesh=mesh,
        in_specs=(
            P(None, None, ("mesh", "sub")),
            device,
            P(),
            P(),
            P(),
            P(),
            P(),
            P(("mesh", "sub"), None, None),
            P(("mesh", "sub"), None, None),
            P(("mesh", "sub"), None, None),
            P(("mesh", "sub"), None, None),
            P(),
            device,
            P(("mesh", "sub"), None),
            device,
            device,
            P("mesh", "sub"),
            P(None, "mesh", "sub"),
            P("mesh", "sub"),
        ),
        out_specs=(P(None, None, ("mesh", "sub")), P("mesh", "sub"), P(None, "mesh", "sub")),
        check_vma=False,
    )
```

time: 42.5 us -> 33.6 us (0.79)
  Pallas kernels: 38.4 us -> 30.8 us
  local copies, waits for them, and re-layouts: 3.28 us -> 1.95 us
    pallas_call x1, Pallas kernels: 38.4 us -> 28.9 us  [body(): pl.pallas_call(functools.partial(kernel, mesh_count, sub_count), out_shap...]
    pallas_call x0 -> x1, Pallas kernels: none -> 1.85 us  [body(): pl.pallas_call(store_kernel, out_shape=tuple((pltpu.HBM(shape, F32) for s...]
    unnamed x7 -> x6, local copies, waits for them, and re-layouts: 3.28 us -> 1.95 us
where the time goes in v2:
time: 33.6 us; the launch traced here: 33.4 us
  Pallas kernels  30.8 us (92%)
  local copies, waits for them, and re-layouts  1.95 us (6%)
  between operations  0.66 us (2%)
    pallas_call x1, Pallas kernels, body(): pl.pallas_call(functools.partial(kernel, mesh_count, sub_count), out_shap...  28.9 us
    unnamed x6, local copies, waits for them, and re-layouts  1.95 us
    pallas_call x1, Pallas kernels, body(): pl.pallas_call(store_kernel, out_shape=tuple((pltpu.HBM(shape, F32) for s...  1.85 us

profile of v2, /device:TPU:1, one launch (start us, length us, event | category | flops | bytes accessed | tf_op | source)
XLA Modules:
  0.0 33.4 jit_solution(3450486745289640338)
XLA Ops:
  0.6 28.9 %shard_map.202 = (f32[504,128]{1,0:T(8,128)S(1)}, f32[64,256]{1,0:T(8,128)S(1)}, f32[2,64,256]{2,1,0:T(8,128)S(1)}) custom-call(f32[504,128]{1,0:T(8,128)} %bitcast.19, f32[1,128]{1,0:T(1,128)} %bitcast.28, f32[168,56]{1,0:T(8,128)} %bitcast.20, f32[9,3,9]{2,1,0:T(4,128)} %bitcast.23, f32[21,4,56]{2,1,0:T(4,128)} %bitcast.21, f32[21,4,56]{2,1,0:T(4,128)} %bitcast.22, ...), custom_call_target="tpu_custom_call" | custom-call | tf_op jit(solution)/shard_map/pallas_call | solution.py:625
  29.6 0.0 copy-start
  29.6 0.7 %copy-done = f32[504,128]{1,0:T(8,128)} copy-done((f32[504,128]{1,0:T(8,128)}, f32[504,128]{1,0:T(8,128)S(1)}, u32[]{:S(2)}) %copy-start) | copy-done | bytes 258072
  30.3 0.0 copy-start.1
  30.3 0.6 %copy-done.1 = f32[2,64,256]{2,1,0:T(8,128)} copy-done((f32[2,64,256]{2,1,0:T(8,128)}, f32[2,64,256]{2,1,0:T(8,128)S(1)}, u32[]{:S(2)}) %copy-start.1) | copy-done | bytes 131096
  30.9 0.0 copy-start.2
  30.9 0.6 %copy-done.2 = f32[64,256]{1,0:T(8,128)} copy-done((f32[64,256]{1,0:T(8,128)}, f32[64,256]{1,0:T(8,128)S(1)}, u32[]{:S(2)}) %copy-start.2) | copy-done | bytes 65560
  31.6 1.9 %shard_map.203 = (f32[504,128]{1,0:T(8,128)}, f32[64,256]{1,0:T(8,128)}, f32[2,64,256]{2,1,0:T(8,128)}) custom-call(f32[504,128]{1,0:T(8,128)} %copy-done, f32[64,256]{1,0:T(8,128)} %copy-done.2, f32[2,64,256]{2,1,0:T(8,128)} %copy-done.1), custom_call_target="tpu_custom_call" | custom-call | tf_op jit(solution)/shard_map/pallas_call | solution.py:635
Async XLA Ops:
  29.6 0.7 %copy-start = (f32[504,128]{1,0:T(8,128)}, f32[504,128]{1,0:T(8,128)S(1)}, u32[]{:S(2)}) copy-start(f32[504,128]{1,0:T(8,128)S(1)} %get-tuple-element.9.new_in) | copy-start | bytes 774148
  30.3 0.6 %copy-start.1 = (f32[2,64,256]{2,1,0:T(8,128)}, f32[2,64,256]{2,1,0:T(8,128)S(1)}, u32[]{:S(2)}) copy-start(f32[2,64,256]{2,1,0:T(8,128)S(1)} %get-tuple-element.11.flow_in) | copy-start | bytes 393220
  30.9 0.6 %copy-start.2 = (f32[64,256]{1,0:T(8,128)}, f32[64,256]{1,0:T(8,128)S(1)}, u32[]{:S(2)}) copy-start(f32[64,256]{1,0:T(8,128)S(1)} %get-tuple-element.10.sea_in) | copy-start | bytes 196612

commit v3 on v2

--- a/solution.py
+++ b/solution.py
@@ -638,7 +638,7 @@
         in_specs=[local] * 3,
         out_specs=(hbm,) * 3,
         scratch_shapes=[dma((3,))],
-    )(*results)
+    )(*[pltpu.with_memory_space_constraint(x, pltpu.VMEM) for x in results])
     new_state = jnp.transpose(new_state.reshape(quantities, basis, elements), (1, 0, 2))
     return new_state, sea_out, flow_out
 

time: 33.6 us -> 30.5 us (0.908)
  local copies, waits for them, and re-layouts: 1.95 us -> 0 us
  Pallas kernels: 30.8 us -> 29.7 us
    unnamed x6 -> x0, local copies, waits for them, and re-layouts: 1.95 us -> none
    pallas_call x1, Pallas kernels: 1.85 us -> 0.79 us  [body(): pl.pallas_call(store_kernel, out_shape=tuple((pltpu.HBM(shape, F32) for s...]
where the time goes in v3:
time: 30.5 us; the launch traced here: 30.4 us
  Pallas kernels  29.7 us (97%)
  between operations  0.65 us (2%)
    pallas_call x1, Pallas kernels, body(): pl.pallas_call(functools.partial(kernel, mesh_count, sub_count), out_shap...  28.9 us
    pallas_call x1, Pallas kernels, body(): pl.pallas_call(store_kernel, out_shape=tuple((pltpu.HBM(shape, F32) for s...  0.79 us

profile of v3, /device:TPU:1, one launch (start us, length us, event | category | flops | bytes accessed | tf_op | source)
XLA Modules:
  0.0 30.4 jit_solution(7672523429944324870)
XLA Ops:
  0.6 28.9 %shard_map.202 = (f32[504,128]{1,0:T(8,128)S(1)}, f32[64,256]{1,0:T(8,128)S(1)}, f32[2,64,256]{2,1,0:T(8,128)S(1)}) custom-call(f32[504,128]{1,0:T(8,128)} %bitcast.19, f32[1,128]{1,0:T(1,128)} %bitcast.28, f32[168,56]{1,0:T(8,128)} %bitcast.20, f32[9,3,9]{2,1,0:T(4,128)} %bitcast.23, f32[21,4,56]{2,1,0:T(4,128)} %bitcast.21, f32[21,4,56]{2,1,0:T(4,128)} %bitcast.22, ...), custom_call_target="tpu_custom_call" | custom-call | tf_op jit(solution)/shard_map/pallas_call | solution.py:625
  29.6 0.8 %shard_map.203 = (f32[504,128]{1,0:T(8,128)}, f32[64,256]{1,0:T(8,128)}, f32[2,64,256]{2,1,0:T(8,128)}) custom-call(f32[504,128]{1,0:T(8,128)S(1)} %get-tuple-element.9.new_in, f32[64,256]{1,0:T(8,128)S(1)} %get-tuple-element.10.sea_in, f32[2,64,256]{2,1,0:T(8,128)S(1)} %get-tuple-element.11.flow_in), custom_call_target="tpu_custom_call" | custom-call | tf_op jit(solution)/shard_map/pallas_call | solution.py:635

commit v4 on v3

--- a/solution.py
+++ b/solution.py
@@ -17,6 +17,7 @@
 FACE_ROWS = 24
 INFO = 224
 RIM = 4
+TURN_LOW, TURN_HIGH = 1, 2
 DIRECTIONS = ((1, 0), (-1, 0), (0, 1), (0, -1), (1, 1), (1, -1), (-1, 1), (-1, -1))
 WAY = {d: i for i, d in enumerate(DIRECTIONS)}
 
@@ -40,10 +41,11 @@
     )
 
 
-def as_column(rows, first=0):
+def as_column(rows, first=0, backward=False):
     count = rows.shape[1] if first == 0 else CAP
     wide = repeat_rows(rows, count)
-    mine = (iota(wide.shape, 0) & (count - 1)) == iota(wide.shape, 1) - first
+    turn = iota(wide.shape, 0) & (count - 1)
+    mine = (count - 1 - turn if backward else turn) == iota(wide.shape, 1) - first
     return jnp.sum(jnp.where(mine, wide, 0.0), axis=1, keepdims=True)
 
 
@@ -99,9 +101,9 @@
         felem, fdest, frow, fslip, sea, vel, depth,
         spread, matrix_hi, matrix_lo, hot, faces, lifts, traces_out, traces_in, items_out, items_in,
         rows_out, cols_out, rows_in, cols_in, corner_in,
-        height, hcols_out, hrows_in, hcols_in, hcorner_in,
+        rims_out, rims_in, sides_out, sides_in,
         load_sem, rim_send, rim_recv, trace_send, trace_recv,
-        item_send, item_recv, high_send, high_recv,
+        item_send, item_recv, side_send, side_recv, edge_send, edge_recv,
     ) = refs
     quantities, basis = flux.shape[0], stiff.shape[1]
     width = quantities * basis
@@ -143,7 +145,7 @@
 
         @pl.when(neighbour[side])
         def _():
-            for ds in (0, 1, -1):
+            for ds in range(sub_count):
                 greet(side, ds)
 
     def remote(src, dst, send_sem, recv_sem, dm, ds):
@@ -244,9 +246,12 @@
         jnp.where(same & (iota(square, 1) < iota(square, 0)), 1.0, 0.0), axis=1, keepdims=True
     )
     row_numbers = frow[...].astype(F32) + 1.0
-    info_left = jnp.where(
-        dest_row == (iota((peer_total, fault_count), 0) // slots).astype(F32), row_numbers, 0.0
-    )
+    info_row = iota((peer_total, 1), 0)
+    info_turn = info_row & (slots - 1)
+    info_dest = info_row // slots + jnp.where(
+        info_turn == TURN_LOW, -1, jnp.where(info_turn == TURN_HIGH, 1, 0)
+    )
+    info_left = jnp.where(dest_row == info_dest.astype(F32), row_numbers, 0.0)
     info_lane = INFO % LANES
     info_right = (
         rank_col == (iota((fault_count, LANES), 1) - info_lane).astype(F32)
@@ -336,7 +341,8 @@
             )
         )
     pl.semaphore_wait(
-        barrier, sub_count - 1 + 3 * (neighbour[1].astype(I32) + neighbour[-1].astype(I32))
+        barrier,
+        sub_count - 1 + sub_count * (neighbour[1].astype(I32) + neighbour[-1].astype(I32)),
     )
     start_all(trace_copies)
     own_block = pltpu.make_async_copy(
@@ -350,11 +356,12 @@
     for i, first in enumerate((tile_rows - 8, 0)):
         rows_out[i, 0:2] = vel[:, first : first + 8, :]
         rows_out[i, 2] = depth[first : first + 8, :]
-    fields = (vel[0], vel[1], depth[...])
+        rows_out[i, 3] = sea[first : first + 8, :]
+    fields = (vel[0], vel[1], depth[...], sea[...])
     group = RIM * (tile_rows // 8)
     for i, last in enumerate((True, False)):
         packed = pack_edge(fields[0], last, 0)
-        for k in (1, 2):
+        for k in (1, 2, 3):
             packed = packed + pack_edge(fields[k], last, k * group)
         cols_out[i] = packed
 
@@ -408,10 +415,27 @@
     ).astype(F32)
     elem_col = as_column(felem[...].astype(F32))
     elem_hot = (elem_col == iota((fault_count, elements), 1).astype(F32)).astype(F32)
-    choose = mm(place.astype(BF16), elem_hot.astype(BF16)).astype(BF16)
-    choose = jnp.concatenate([choose, choose], 1)
+    elem_hot = elem_hot.astype(BF16)
+    choose = mm(place.astype(BF16), elem_hot).astype(BF16)
     weighting = 0.3 + 0.7 * fslip[...].astype(F32)
     weight_col = jnp.sum(place * weighting, axis=1, keepdims=True)
+    rim_total = 2 * sub_count * RIM
+    rim_row = iota((rim_total, 1), 0)
+    rim_turn = rim_row & (RIM - 1)
+    upward = rim_row >= rim_total // 2
+    rim_target = jnp.where(
+        upward,
+        jnp.where(rim_turn > 0, tile_rows - RIM + rim_turn, -1),
+        jnp.where(rim_turn < RIM - 1, rim_turn, -1),
+    )
+    rim_dest = (rim_row & (rim_total // 2 - 1)) // RIM
+    rim_weight = jnp.where(
+        (dest_row == rim_dest.astype(F32)) & (frow[...] == rim_target), weighting, 0.0
+    )
+    rim_hi, rim_lo = split(rim_weight)
+    rim_hi, rim_lo = split(mm(rim_hi, elem_hot) + mm(rim_lo, elem_hot))
+    choose = jnp.concatenate([choose, rim_hi], 0)
+    choose = jnp.concatenate([choose, choose], 1)
 
     own_block.wait()
     received_all(trace_copies)
@@ -447,10 +471,50 @@
     new_state = base + face_sum
     new_out[...] = new_state[0:width]
 
-    columns = mm(choose, jnp.concatenate(split(new_state), 1), 1, 1)
+    new_hi, new_lo = split(new_state)
+    columns = mm(choose, jnp.concatenate([new_hi, new_lo], 1), 1, 1)
+    columns = jnp.concatenate(
+        [columns[:item_slots], columns[item_slots:] + mm(rim_lo, new_hi, 1, 1)], 0
+    )
     columns_hi, columns_lo = split(columns)
-    items = mm(columns_hi, uplift_hi) + mm(columns_lo, uplift_hi) + mm(columns_hi, uplift_lo)
-    items_out[...] = items * weight_col
+    uplifted = mm(columns_hi, uplift_hi) + mm(columns_lo, uplift_hi) + mm(columns_hi, uplift_lo)
+    rims = uplifted[item_slots:]
+    half = rim_total // 2
+    rim_lane = iota((half, LANES), 1)
+    for i, (part, high_shift, low_shift) in enumerate(
+        ((rims[:half], -RIM, RIM), (rims[half:], 1 - 2 * RIM, 1))
+    ):
+        corner = []
+        for shift, tile in (
+            (high_shift, jnp.where(rim_lane < RIM - 1, part[:, 0:LANES], 0.0)),
+            (low_shift, jnp.where(rim_lane > LANES - RIM, part[:, tile_cols - LANES :], 0.0)),
+        ):
+            tile = pltpu.roll(tile, 0, 1, stride=8, stride_axis=0)
+            tile = tile + pltpu.roll(tile, 1, 0)
+            tile = tile + pltpu.roll(tile, 2, 0)
+            corner.append(pltpu.roll(tile, shift % half, 0))
+        free = (iota((half, LANES), 0) & (RIM - 1)) == (0 if i else RIM - 1)
+        first = jnp.where(free, corner[0] + corner[1], part[:, 0:LANES])
+        for d in range(sub_count):
+            rims_out[i, d, :, 0:LANES] = first[d * RIM : (d + 1) * RIM]
+            rims_out[i, d, :, LANES:] = part[d * RIM : (d + 1) * RIM, LANES:]
+
+    edge_copies = []
+    for k in [*order, 0]:
+        _, peer = device(0, k)
+        for i, dm in enumerate((-1, 1)):
+            edge_copies.append(
+                (
+                    dm,
+                    remote(
+                        rims_out.at[i, peer], rims_in.at[i, sub],
+                        edge_send.at[i, k], edge_recv.at[i, k], dm, k,
+                    ),
+                )
+            )
+    start_all(edge_copies)
+    items = uplifted[:item_slots] * weight_col
+    items_out[...] = items
     item_copies = []
     for k in order:
         _, peer = device(0, k)
@@ -468,28 +532,61 @@
         items_out.at[peer_block(sub, CAP), :], items_in.at[peer_block(sub, CAP), :], item_recv.at[0]
     )
     own_items.start()
+    side_lane = iota((CAP, LANES), 1)
+    firsts, lasts = [], []
+    for d in range(sub_count):
+        own = items[d * CAP : (d + 1) * CAP]
+        first = jnp.where(side_lane < RIM - 1, own[:, 0:LANES], 0.0)
+        last = jnp.where(side_lane > LANES - RIM, own[:, tile_cols - LANES :], 0.0)
+        first = pltpu.roll(first, 0, 1, stride=RIM, stride_axis=0)
+        last = pltpu.roll(last, LANES // 2 + RIM - 1, 1, stride=RIM, stride_axis=0)
+        firsts.append(jnp.sum(first, axis=0, keepdims=True))
+        lasts.append(jnp.sum(last, axis=0, keepdims=True))
+    for d in range(sub_count):
+        sides_out[d] = firsts[(d + 1) % sub_count] + lasts[(d - 1) % sub_count]
+    side_copies = []
+    for k in order:
+        _, peer = device(0, k)
+        side_copies.append(
+            (
+                0,
+                remote(
+                    sides_out.at[peer], sides_in.at[sub], side_send.at[k], side_recv.at[k], 0, k
+                ),
+            )
+        )
+    start_all(side_copies)
+    own_side = pltpu.make_async_copy(sides_out.at[sub], sides_in.at[sub], side_recv.at[0])
+    own_side.start()
 
     got_info = traces_in[0:peer_total, LANES:]
-    first_rows = jnp.concatenate([got_info[s * slots : s * slots + 1] for s in range(sub_count)], 0)
-    landing_col = as_column(first_rows, info_lane)
-    landing = (landing_col == iota((item_slots, LANES), 1).astype(F32)).astype(F32)
-    landing = jnp.transpose(landing)[0:tile_rows].astype(BF16)
-    landing = jnp.concatenate([landing, landing], 1)
+
+    def landing(turn, backward=False):
+        rows = jnp.concatenate(
+            [got_info[s * slots + turn : s * slots + turn + 1] for s in range(sub_count)], 0
+        )
+        column = as_column(rows, info_lane, backward)
+        hits = (column == iota((item_slots, LANES), 1).astype(F32)).astype(F32)
+        return jnp.transpose(hits)[0:tile_rows].astype(BF16)
+
+    land = landing(0)
+    land = jnp.concatenate([land, land], 1)
+    land_high, land_low = landing(TURN_HIGH, True), landing(TURN_LOW, True)
+    land_side = jnp.concatenate([land_high, land_low, land_high, land_low], 1)
 
     received_all(field_copies)
 
-    def corners_of(ref, k=None):
+    def corners_of(k):
         return [
-            ref[WAY[way] - 4] if k is None else ref[WAY[way] - 4, k]
-            for way in ((-1, -1), (-1, 1), (1, -1), (1, 1))
+            corner_in[WAY[way] - 4, k] for way in ((-1, -1), (-1, 1), (1, -1), (1, 1))
         ]
 
     extended = [
         extend(
             fields[k], rows_in[WAY[(1, 0)], k], rows_in[WAY[(-1, 0)], k],
-            cols_in[0], cols_in[1], corners_of(corner_in, k), k * group,
-        )
-        for k in range(3)
+            cols_in[0], cols_in[1], corners_of(k), k * group,
+        )
+        for k in range(4)
     ]
     shape = extended[0].shape
     ext_row, ext_lane = iota(shape, 0), iota(shape, 1)
@@ -501,33 +598,58 @@
     )
     flow = [jnp.where(inside, extended[axis], 0.0) for axis in (0, 1)]
     deep = jnp.where(inside, extended[2], 0.0)
-    change = COURANT * (shifted(deep * flow[0], 0) + shifted(deep * flow[1], 1))
+    calm = jnp.where(inside, extended[3], 0.0) - COURANT * (
+        shifted(deep * flow[0], 0) + shifted(deep * flow[1], 1)
+    )
+    for copies in (trace_copies, field_copies):
+        sent_all(copies)
+
+    own_side.wait()
+    received_all(side_copies)
+    beside = []
+    last_turn = LANES - RIM * (CAP - 1)
+    for shift, keep in (
+        (last_turn, side_lane < RIM - 1),
+        (last_turn + LANES // 2 - RIM + 1, side_lane > LANES - RIM),
+    ):
+        for s in range(sub_count):
+            wide = jnp.broadcast_to(sides_in[s], (CAP, LANES))
+            wide = pltpu.roll(wide, shift % LANES, 1, stride=RIM, stride_axis=0)
+            beside.append(jnp.where(keep, wide, 0.0))
+    beside_hi, beside_lo = split(jnp.concatenate(beside, 0))
+    side = mm(land_side, jnp.concatenate([beside_hi, beside_lo], 0))
 
     own_items.wait()
     received_all(item_copies)
-    deposit = mm(landing, jnp.concatenate(split(items_in[...]), 0))
-    level = sea[...] + deposit
-    height[...] = level
-    hcols_out[0] = pack_edge(level, True, 0)
-    hcols_out[1] = pack_edge(level, False, 0)
-
-    def rows_of_height(dm, lanes):
-        rows = slice(tile_rows - 8, tile_rows) if dm > 0 else slice(0, 8)
-        return height.at[rows, :] if lanes is None else height.at[rows, lanes]
-
-    high_copies = rim_copies(
-        rows_of_height, hcols_out, hrows_in, hcols_in, hcorner_in, high_send, high_recv
-    )
-    start_all(high_copies)
-    for copies in (trace_copies, field_copies, item_copies):
-        sent_all(copies)
-
-    received_all(high_copies)
-    level = extend(
-        level, hrows_in[WAY[(1, 0)]], hrows_in[WAY[(-1, 0)]], hcols_in[0], hcols_in[1],
-        corners_of(hcorner_in), 0,
-    )
-    level = jnp.where(inside, level, 0.0) - change
+    received_all(edge_copies)
+    deposit = mm(land, jnp.concatenate(split(items_in[...]), 0))
+    bottom = []
+    for i in (0, 1):
+        total = rims_in[i, 0]
+        for s in range(1, sub_count):
+            total = total + rims_in[i, s]
+        bottom.append(total)
+    bottom = jnp.concatenate(bottom, 0)
+    bottom_lane, bottom_row = iota((8, LANES), 1), iota((8, LANES), 0)
+    corner = []
+    for free in (RIM - 1, RIM):
+        wide = jnp.broadcast_to(bottom[free : free + 1, 0:LANES], (8, LANES))
+        around = []
+        for turn in (1, -1):
+            tile = pltpu.roll(wide, lax.rem(8 * LANES - 8 * RIM * (sub + turn), LANES), 1)
+            rows = tile
+            for r in range(1, RIM):
+                rows = jnp.where(
+                    (bottom_row & (RIM - 1)) == r, pltpu.roll(tile, LANES - 8 * r, 1), rows
+                )
+            around.append(rows)
+        corner.append(jnp.where(bottom_lane < LANES // 2, around[0], around[1]))
+    corner = jnp.where(bottom_row < RIM, corner[0], corner[1])
+    raised = jnp.concatenate(
+        [jnp.concatenate([deposit, side], 1), jnp.concatenate([bottom, corner], 1)], 0
+    )
+
+    level = calm + jnp.where(inside, raised, 0.0)
     flow = [flow[axis] - COURANT * shifted(level, axis) for axis in (0, 1)]
     level = jnp.where(inside, level, 0.0)
     level = level - COURANT * (shifted(deep * flow[0], 0) + shifted(deep * flow[1], 1))
@@ -535,7 +657,8 @@
     sea_out[...] = level[0:tile_rows, 0:tile_cols]
     flow_out[0] = flow[0][0:tile_rows, 0:tile_cols]
     flow_out[1] = flow[1][0:tile_rows, 0:tile_cols]
-    sent_all(high_copies)
+    for copies in (edge_copies, item_copies, side_copies):
+        sent_all(copies)
 
 
 def store_kernel(new_in, sea_in, flow_in, new_out, sea_out, flow_out, sems):
@@ -600,16 +723,15 @@
         vmem((send_total, trace_lanes), F32),
         vmem((item_slots, cols), F32),
         vmem((item_slots, cols), F32),
-        vmem((2, 3, 8, cols), F32),
+        vmem((2, 4, 8, cols), F32),
         vmem((2, 8, LANES), F32),
-        vmem((2, 3, 8, cols), F32),
+        vmem((2, 4, 8, cols), F32),
         vmem((2, 8, LANES), F32),
-        vmem((4, 3, 8, LANES), F32),
-        vmem((rows, cols), F32),
-        vmem((2, 8, LANES), F32),
-        vmem((2, 8, cols), F32),
-        vmem((2, 8, LANES), F32),
-        vmem((4, 8, LANES), F32),
+        vmem((4, 4, 8, LANES), F32),
+        vmem((2, sub_count, RIM, cols), F32),
+        vmem((2, sub_count, RIM, cols), F32),
+        vmem((sub_count, 1, LANES), F32),
+        vmem((sub_count, 1, LANES), F32),
         dma((len(operands),)),
         dma((8,)),
         dma((8,)),
@@ -617,8 +739,10 @@
         dma((sub_count + 2,)),
         dma((sub_count,)),
         dma((sub_count,)),
-        dma((8,)),
-        dma((8,)),
+        dma((sub_count,)),
+        dma((sub_count,)),
+        dma((2, sub_count)),
+        dma((2, sub_count)),
     ]
     hbm, local = pl.BlockSpec(memory_space=pltpu.HBM), pl.BlockSpec(memory_space=pltpu.VMEM)
     shapes = ((width, elements), (rows, cols), (2, rows, cols))

time: 30.5 us -> 28.1 us (0.921)
  Pallas kernels: 29.7 us -> 27.2 us
    pallas_call x1, Pallas kernels: 28.9 us -> 26.4 us  [body(): pl.pallas_call(functools.partial(kernel, mesh_count, sub_count), out_shap...]
where the time goes in v4:
time: 28.1 us; the launch traced here: 27.9 us
  Pallas kernels  27.2 us (97%)
  between operations  0.65 us (2%)
    pallas_call x1, Pallas kernels, body(): pl.pallas_call(functools.partial(kernel, mesh_count, sub_count), out_shap...  26.4 us
    pallas_call x1, Pallas kernels, body(): pl.pallas_call(store_kernel, out_shape=tuple((pltpu.HBM(shape, F32) for s...  0.79 us

profile of v4, /device:TPU:1, one launch (start us, length us, event | category | flops | bytes accessed | tf_op | source)
XLA Modules:
  0.0 27.9 jit_solution(4754969773409421820)
XLA Ops:
  0.6 26.4 %shard_map.202 = (f32[504,128]{1,0:T(8,128)S(1)}, f32[64,256]{1,0:T(8,128)S(1)}, f32[2,64,256]{2,1,0:T(8,128)S(1)}) custom-call(f32[504,128]{1,0:T(8,128)} %bitcast.19, f32[1,128]{1,0:T(1,128)} %bitcast.28, f32[168,56]{1,0:T(8,128)} %bitcast.20, f32[9,3,9]{2,1,0:T(4,128)} %bitcast.23, f32[21,4,56]{2,1,0:T(4,128)} %bitcast.21, f32[21,4,56]{2,1,0:T(4,128)} %bitcast.22, ...), custom_call_target="tpu_custom_call" | custom-call | tf_op jit(solution)/shard_map/pallas_call | solution.py:749
  27.1 0.8 %shard_map.203 = (f32[504,128]{1,0:T(8,128)}, f32[64,256]{1,0:T(8,128)}, f32[2,64,256]{2,1,0:T(8,128)}) custom-call(f32[504,128]{1,0:T(8,128)S(1)} %get-tuple-element.9.new_in, f32[64,256]{1,0:T(8,128)S(1)} %get-tuple-element.10.sea_in, f32[2,64,256]{2,1,0:T(8,128)S(1)} %get-tuple-element.11.flow_in), custom_call_target="tpu_custom_call" | custom-call | tf_op jit(solution)/shard_map/pallas_call | solution.py:759

commit v5 on v4

--- a/solution.py
+++ b/solution.py
@@ -17,6 +17,7 @@
 FACE_ROWS = 24
 INFO = 224
 RIM = 4
+TRACES, FIELDS, RIMS, ITEMS, SIDES = range(5)
 TURN_LOW, TURN_HIGH = 1, 2
 DIRECTIONS = ((1, 0), (-1, 0), (0, 1), (0, -1), (1, 1), (1, -1), (-1, 1), (-1, -1))
 WAY = {d: i for i, d in enumerate(DIRECTIONS)}
@@ -102,8 +103,7 @@
         spread, matrix_hi, matrix_lo, hot, faces, lifts, traces_out, traces_in, items_out, items_in,
         rows_out, cols_out, rows_in, cols_in, corner_in,
         rims_out, rims_in, sides_out, sides_in,
-        load_sem, rim_send, rim_recv, trace_send, trace_recv,
-        item_send, item_recv, side_send, side_recv, edge_send, edge_recv,
+        known, mixing_hi, mixing_lo, load_sem, recv_sem,
     ) = refs
     quantities, basis = flux.shape[0], stiff.shape[1]
     width = quantities * basis
@@ -148,46 +148,47 @@
             for ds in range(sub_count):
                 greet(side, ds)
 
-    def remote(src, dst, send_sem, recv_sem, dm, ds):
-        return pltpu.make_async_remote_copy(
-            src_ref=src, dst_ref=dst, send_sem=send_sem, recv_sem=recv_sem,
-            device_id=device(dm, ds), device_id_type=MESH,
-        )
-
-    def each(copies, act):
-        for dm, copy in copies:
-            if dm == 0:
-                act(copy)
+    def start(group, copies):
+        for side in (0, 1, -1):
+            some = [copy for copy in copies if copy[0] == side]
+
+            def go():
+                for dm, ds, src, dst in some:
+                    pltpu.make_async_remote_copy(
+                        src_ref=src, dst_ref=dst,
+                        send_sem=load_sem.at[3 * group + side % 3],
+                        recv_sem=recv_sem.at[3 * group + side % 3],
+                        device_id=device(dm, ds), device_id_type=MESH,
+                    ).start()
+
+            if side == 0:
+                go()
+            elif some:
+                pl.when(neighbour[side])(go)
+
+    def await_all(sem, whole):
+        pltpu.make_async_copy(whole, whole, sem).wait()
+
+    def sent(group, along, across):
+        if along is not None:
+            await_all(load_sem.at[3 * group], along)
         for side in (1, -1):
-            some = [copy for dm, copy in copies if dm == side]
-            if some:
-
-                @pl.when(neighbour[side])
-                def _():
-                    for copy in some:
-                        act(copy)
-
-    def start_all(copies):
-        each(copies, lambda copy: copy.start())
-
-    def sent_all(copies):
-        each(copies, lambda copy: copy.wait_send())
-
-    def received_all(copies):
-        each([(-dm, copy) for dm, copy in copies], lambda copy: copy.wait_recv())
-
-    def rim_copies(rows_of, cols_ref, rows_ref, cols_got, corner_ref, send_sem, recv_sem):
-        copies = []
-        for i, (dm, ds) in enumerate(DIRECTIONS):
-            if ds == 0:
-                src, dst = rows_of(dm, None), rows_ref.at[i]
-            elif dm == 0:
-                src, dst = cols_ref.at[i - 2], cols_got.at[i - 2]
-            else:
-                lanes = slice(tile_cols - LANES, tile_cols) if ds > 0 else slice(0, LANES)
-                src, dst = rows_of(dm, lanes), corner_ref.at[i - 4]
-            copies.append((dm, remote(src, dst, send_sem.at[i], recv_sem.at[i], dm, ds)))
-        return copies
+            if across is not None:
+                pl.when(neighbour[side])(
+                    functools.partial(await_all, load_sem.at[3 * group + side % 3], across)
+                )
+
+    def received(group, along, across):
+        if along is not None:
+            await_all(recv_sem.at[3 * group], along)
+        for side in (1, -1):
+            if across is not None:
+                pl.when(neighbour[-side])(
+                    functools.partial(await_all, recv_sem.at[3 * group + side % 3], across)
+                )
+
+    def keep_own(group, src, dst):
+        pltpu.make_async_copy(src, dst, recv_sem.at[3 * group]).start()
 
     lane = iota((1, padded), 1)
     of_quantity = sum((lane >= basis * k).astype(I32) for k in range(1, quantities + 1))
@@ -221,6 +222,18 @@
         matrix_lo[at : at + high.shape[0], :] = low
         at = at + high.shape[0]
 
+    scale = scales[...]
+
+    def derivative(x):
+        x_hi, x_lo = split(x)
+        both = mm(matrix_hi[...], jnp.concatenate([x_hi, x_lo], 1))
+        return (both[:, :elements] + both[:, elements:] + mm(matrix_lo[...], x_hi)) * scale
+
+    start_state = jnp.concatenate([state[...], jnp.zeros((padded - width, elements), F32)], 0)
+    current = derivative(start_state)
+    factor = EARTH_STEP * EARTH_STEP / 2
+    integral = EARTH_STEP * start_state + factor * current
+
     codes = jnp.concatenate(
         [as_column(ref[...].astype(F32)) for ref in (psend, esend, precv, erecv)], 0
     )
@@ -260,18 +273,7 @@
     info_lanes = iota((peer_total, LANES), 1)
     info_here = (info_lanes >= info_lane) & (info_lanes < info_lane + CAP)
 
-    scale = scales[...]
-
-    def derivative(x):
-        x_hi, x_lo = split(x)
-        both = mm(matrix_hi[...], jnp.concatenate([x_hi, x_lo], 1))
-        return (both[:, :elements] + both[:, elements:] + mm(matrix_lo[...], x_hi)) * scale
-
-    start = jnp.concatenate([state[...], jnp.zeros((padded - width, elements), F32)], 0)
-    factor = EARTH_STEP
-    integral = factor * start
-    current = start
-    for power in range(1, ORDER):
+    for power in range(2, ORDER):
         current = derivative(current)
         factor = factor * EARTH_STEP / (power + 1)
         integral = integral + factor * current
@@ -319,37 +321,28 @@
         _, peer = device(0, k)
         trace_copies.append(
             (
-                0,
-                remote(
-                    traces_out.at[peer_block(peer, slots), :],
-                    traces_in.at[peer_block(sub, slots), :],
-                    trace_send.at[k], trace_recv.at[k], 0, k,
-                ),
+                0, k,
+                traces_out.at[peer_block(peer, slots), :], traces_in.at[peer_block(sub, slots), :],
             )
         )
-    for i, dm in enumerate((1, -1)):
+    for dm in (1, -1):
         source = peer_total + (edge_slots if dm > 0 else 0)
         target = peer_total + (0 if dm > 0 else edge_slots)
         trace_copies.append(
             (
-                dm,
-                remote(
-                    traces_out.at[source : source + edge_slots, :],
-                    traces_in.at[target : target + edge_slots, :],
-                    trace_send.at[sub_count + i], trace_recv.at[sub_count + i], dm, 0,
-                ),
+                dm, 0,
+                traces_out.at[source : source + edge_slots, :],
+                traces_in.at[target : target + edge_slots, :],
             )
         )
     pl.semaphore_wait(
         barrier,
         sub_count - 1 + sub_count * (neighbour[1].astype(I32) + neighbour[-1].astype(I32)),
     )
-    start_all(trace_copies)
-    own_block = pltpu.make_async_copy(
-        traces_out.at[peer_block(sub, slots), :], traces_in.at[peer_block(sub, slots), :],
-        trace_recv.at[0],
-    )
-    own_block.start()
+    start(TRACES, trace_copies)
+    keep_own(
+        TRACES, traces_out.at[peer_block(sub, slots), :], traces_in.at[peer_block(sub, slots), :]
+    )
 
     for load in loads[15:]:
         load.wait()
@@ -365,23 +358,26 @@
             packed = packed + pack_edge(fields[k], last, k * group)
         cols_out[i] = packed
 
-    def rows_of_fields(dm, lanes):
-        i = 0 if dm > 0 else 1
-        return rows_out.at[i] if lanes is None else rows_out.at[i, :, :, lanes]
-
-    field_copies = rim_copies(
-        rows_of_fields, cols_out, rows_in, cols_in, corner_in, rim_send, rim_recv
-    )
-    start_all(field_copies)
-
-    base = start + derivative(integral)
+    rim_copies = []
+    for i, (dm, ds) in enumerate(DIRECTIONS):
+        if ds == 0:
+            src, dst = rows_out.at[i], rows_in.at[i]
+        elif dm == 0:
+            src, dst = cols_out.at[i - 2], cols_in.at[i - 2]
+        else:
+            lanes = slice(tile_cols - LANES, tile_cols) if ds > 0 else slice(0, LANES)
+            src, dst = rows_out.at[0 if dm > 0 else 1, :, :, lanes], corner_in.at[i - 4]
+        rim_copies.append((dm, ds, src, dst))
+    start(FIELDS, rim_copies)
+
+    base = start_state + derivative(integral)
     lifts[...] = jnp.zeros(lifts.shape, F32)
     for f in range(4):
-        lifts[f * FACE_ROWS : f * FACE_ROWS + lift.shape[0], :] = lift[:, f, :]
-    lift_hi, lift_lo = split(jnp.transpose(lifts[...]))
+        for at in (0, LANES // 2):
+            lifts[f * FACE_ROWS : f * FACE_ROWS + lift.shape[0], at : at + basis] = lift[:, f, :]
+    lift_hi, lift_lo = split(jnp.transpose(lifts[...])[0:basis])
     lift_hi = jnp.concatenate([lift_hi, lift_hi], 1)
     hot_in = hot[send_total:, :]
-    hot_in = jnp.concatenate([hot_in, hot_in], 0)
 
     face_col, face_row = iota((trace_rows, 1), 0), iota((1, trace_rows), 1)
     quantity_col = sum((face_col >= FACE_ROWS * k).astype(I32) for k in range(1, quantities + 1))
@@ -398,7 +394,8 @@
         (((1,), (0,)), ((), ())),
     )
     same_face = face_col - FACE_ROWS * quantity_col == face_row - FACE_ROWS * quantity_row
-    flux_hi, flux_lo = split(jnp.where(same_face, flux_wide, 0.0))
+    flux_wide = jnp.where(same_face, flux_wide, 0.0)
+    flux_hi, flux_lo = split(flux_wide)
 
     rows_here = iota((padded, 1), 0)
     row_quantity = sum((rows_here >= basis * k).astype(I32) for k in range(1, quantities + 1))
@@ -406,8 +403,40 @@
     wanted = jnp.where(rows_here < width, wanted, -1)
     permute = (iota((padded, width), 1) == wanted).astype(F32).astype(BF16)
     uplift_hi, uplift_lo = split(uplift[...])
-    uplift_hi = mm(permute, uplift_hi).astype(BF16)
-    uplift_lo = mm(permute, uplift_lo).astype(BF16)
+    uplift_hi, uplift_lo = mm(permute, uplift_hi), mm(permute, uplift_lo)
+    uplift_all = uplift_hi + uplift_lo
+    uplift_hi, uplift_lo = uplift_hi.astype(BF16), uplift_lo.astype(BF16)
+
+    wide_hi, wide_lo = split(
+        jnp.concatenate(
+            [
+                jnp.concatenate(
+                    [
+                        uplift_all[q * basis : (q + 1) * basis],
+                        jnp.zeros((LANES // 2 - basis, tile_cols), F32),
+                    ],
+                    0,
+                )
+                for q in range(quantities)
+            ],
+            1,
+        )
+    )
+    down_hi, down_lo = split(lifts[...])
+    faces_up = mm(down_hi, jnp.concatenate([wide_hi, wide_lo], 0))
+    faces_up = faces_up + mm(down_lo[:, 0 : LANES // 2], wide_hi)
+    back_hi, back_lo = split(jnp.transpose(flux_wide))
+    for f in range(4):
+        rows = [
+            faces_up[f * FACE_ROWS : (f + 1) * FACE_ROWS, q * tile_cols : (q + 1) * tile_cols]
+            for q in range(quantities)
+        ]
+        rows.append(jnp.zeros((trace_rows - face_width, tile_cols), F32))
+        rows_hi, rows_lo = split(jnp.concatenate(rows, 0))
+        block = mm(back_hi, rows_hi) + mm(back_lo, rows_hi) + mm(back_hi, rows_lo)
+        high, low = split(block)
+        mixing_hi[f * trace_rows : (f + 1) * trace_rows, :] = high
+        mixing_lo[f * trace_rows : (f + 1) * trace_rows, :] = low
 
     item_slots = sub_count * CAP
     place = (
@@ -434,50 +463,44 @@
     )
     rim_hi, rim_lo = split(rim_weight)
     rim_hi, rim_lo = split(mm(rim_hi, elem_hot) + mm(rim_lo, elem_hot))
-    choose = jnp.concatenate([choose, rim_hi], 0)
-    choose = jnp.concatenate([choose, choose], 1)
-
-    own_block.wait()
-    received_all(trace_copies)
+
+    base_hi, base_lo = split(base)
+    both = jnp.concatenate([choose, rim_hi], 0)
+    columns = mm(jnp.concatenate([both, both], 1), jnp.concatenate([base_hi, base_lo], 1), 1, 1)
+    columns = jnp.concatenate(
+        [columns[:item_slots], columns[item_slots:] + mm(rim_lo, base_hi, 1, 1)], 0
+    )
+    columns_hi, columns_lo = split(columns)
+    known[...] = mm(columns_hi, uplift_hi) + mm(columns_lo, uplift_hi) + mm(columns_hi, uplift_lo)
+    in_codes = codes[send_total:].astype(I32)
+    in_elem = jnp.where(in_codes >= 0, in_codes >> 2, -1)
+    in_hot = (in_elem == iota((send_total, elements), 1)).astype(F32).astype(BF16)
+    touch = mm(choose, in_hot, 1, 1).astype(BF16)
+    touch_hi, touch_lo = split(mm(rim_hi, in_hot, 1, 1) + mm(rim_lo, in_hot, 1, 1))
+    touch = jnp.concatenate([touch, touch_hi], 0)
+    touch = jnp.concatenate([touch, touch], 1)
+    turns = [
+        jnp.broadcast_to(((in_codes >= 0) & ((in_codes & 3) == f)).astype(F32), own_trace.shape)
+        .astype(BF16)
+        for f in range(4)
+    ]
+
+    received(TRACES, traces_in.at[0:peer_total, :], traces_in.at[0:edge_slots, :])
     slot_col = iota((send_total, 1), 0)
     missing = ((slot_col >= peer_total) & (slot_col < peer_total + edge_slots) & (me == 0)) | (
         (slot_col >= peer_total + edge_slots) & (me == mesh_count - 1)
     )
     difference = jnp.where(missing, 0.0, traces_in[...]) - own_trace
     diff_hi, diff_lo = split(difference)
-    mixed = mm(flux_hi, jnp.concatenate([diff_hi, diff_lo], 0), 1, 1)
-    mixed = mixed[:, :send_total] + mixed[:, send_total:] + mm(flux_lo, diff_hi, 1, 1)
-    scattered = mm(jnp.concatenate(split(mixed), 1), hot_in)
-    gathered = jnp.concatenate(
-        [
-            jnp.concatenate(
-                [
-                    scattered[q * FACE_ROWS : (q + 1) * FACE_ROWS, f * elements : (f + 1) * elements]
-                    for f in range(4)
-                ],
-                0,
-            )
-            for q in range(quantities)
-        ],
-        1,
-    )
-    gathered_hi, gathered_lo = split(gathered)
-    lifted = mm(lift_hi, jnp.concatenate([gathered_hi, gathered_lo], 0)) + mm(lift_lo, gathered_hi)
-    face_sum = jnp.concatenate(
-        [lifted[:, q * elements : (q + 1) * elements] for q in range(quantities)]
-        + [jnp.zeros((padded - width, elements), F32)],
-        0,
-    )
-    new_state = base + face_sum
-    new_out[...] = new_state[0:width]
-
-    new_hi, new_lo = split(new_state)
-    columns = mm(choose, jnp.concatenate([new_hi, new_lo], 1), 1, 1)
-    columns = jnp.concatenate(
-        [columns[:item_slots], columns[item_slots:] + mm(rim_lo, new_hi, 1, 1)], 0
-    )
-    columns_hi, columns_lo = split(columns)
-    uplifted = mm(columns_hi, uplift_hi) + mm(columns_lo, uplift_hi) + mm(columns_hi, uplift_lo)
+    turned_hi = jnp.concatenate([diff_hi * turn for turn in turns], 1)
+    turned_lo = jnp.concatenate([diff_lo * turn for turn in turns], 1)
+    each_hi, each_lo = split(
+        mm(turned_hi, mixing_hi[...]) + mm(turned_lo, mixing_hi[...]) + mm(turned_hi, mixing_lo[...])
+    )
+    uplifted = known[...] + mm(touch, jnp.concatenate([each_hi, each_lo], 0))
+    uplifted = jnp.concatenate(
+        [uplifted[:item_slots], uplifted[item_slots:] + mm(touch_lo, each_hi)], 0
+    )
     rims = uplifted[item_slots:]
     half = rim_total // 2
     rim_lane = iota((half, LANES), 1)
@@ -499,39 +522,26 @@
             rims_out[i, d, :, 0:LANES] = first[d * RIM : (d + 1) * RIM]
             rims_out[i, d, :, LANES:] = part[d * RIM : (d + 1) * RIM, LANES:]
 
-    edge_copies = []
+    rim_copies = []
     for k in [*order, 0]:
         _, peer = device(0, k)
         for i, dm in enumerate((-1, 1)):
-            edge_copies.append(
-                (
-                    dm,
-                    remote(
-                        rims_out.at[i, peer], rims_in.at[i, sub],
-                        edge_send.at[i, k], edge_recv.at[i, k], dm, k,
-                    ),
-                )
-            )
-    start_all(edge_copies)
+            rim_copies.append((dm, k, rims_out.at[i, peer], rims_in.at[i, sub]))
+    start(RIMS, rim_copies)
     items = uplifted[:item_slots] * weight_col
     items_out[...] = items
-    item_copies = []
-    for k in order:
-        _, peer = device(0, k)
-        item_copies.append(
+    start(
+        ITEMS,
+        [
             (
-                0,
-                remote(
-                    items_out.at[peer_block(peer, CAP), :], items_in.at[peer_block(sub, CAP), :],
-                    item_send.at[k], item_recv.at[k], 0, k,
-                ),
+                0, k,
+                items_out.at[peer_block(device(0, k)[1], CAP), :],
+                items_in.at[peer_block(sub, CAP), :],
             )
-        )
-    start_all(item_copies)
-    own_items = pltpu.make_async_copy(
-        items_out.at[peer_block(sub, CAP), :], items_in.at[peer_block(sub, CAP), :], item_recv.at[0]
-    )
-    own_items.start()
+            for k in order
+        ],
+    )
+    keep_own(ITEMS, items_out.at[peer_block(sub, CAP), :], items_in.at[peer_block(sub, CAP), :])
     side_lane = iota((CAP, LANES), 1)
     firsts, lasts = [], []
     for d in range(sub_count):
@@ -544,20 +554,35 @@
         lasts.append(jnp.sum(last, axis=0, keepdims=True))
     for d in range(sub_count):
         sides_out[d] = firsts[(d + 1) % sub_count] + lasts[(d - 1) % sub_count]
-    side_copies = []
-    for k in order:
-        _, peer = device(0, k)
-        side_copies.append(
-            (
+    start(
+        SIDES, [(0, k, sides_out.at[device(0, k)[1]], sides_in.at[sub]) for k in order]
+    )
+    keep_own(SIDES, sides_out.at[sub], sides_in.at[sub])
+
+    mixed = mm(flux_hi, jnp.concatenate([diff_hi, diff_lo], 0), 1, 1)
+    mixed = mixed[:, :send_total] + mixed[:, send_total:] + mm(flux_lo, diff_hi, 1, 1)
+    scattered = mm(jnp.concatenate(split(mixed), 1), jnp.concatenate([hot_in, hot_in], 0))
+    gathered = jnp.concatenate(
+        [
+            jnp.concatenate(
+                [
+                    scattered[q * FACE_ROWS : (q + 1) * FACE_ROWS, f * elements : (f + 1) * elements]
+                    for f in range(4)
+                ],
                 0,
-                remote(
-                    sides_out.at[peer], sides_in.at[sub], side_send.at[k], side_recv.at[k], 0, k
-                ),
             )
-        )
-    start_all(side_copies)
-    own_side = pltpu.make_async_copy(sides_out.at[sub], sides_in.at[sub], side_recv.at[0])
-    own_side.start()
+            for q in range(quantities)
+        ],
+        1,
+    )
+    gathered_hi, gathered_lo = split(gathered)
+    lifted = mm(lift_hi, jnp.concatenate([gathered_hi, gathered_lo], 0)) + mm(lift_lo, gathered_hi)
+    face_sum = jnp.concatenate(
+        [lifted[:, q * elements : (q + 1) * elements] for q in range(quantities)]
+        + [jnp.zeros((padded - width, elements), F32)],
+        0,
+    )
+    new_out[...] = (base + face_sum)[0:width]
 
     got_info = traces_in[0:peer_total, LANES:]
 
@@ -574,7 +599,7 @@
     land_high, land_low = landing(TURN_HIGH, True), landing(TURN_LOW, True)
     land_side = jnp.concatenate([land_high, land_low, land_high, land_low], 1)
 
-    received_all(field_copies)
+    received(FIELDS, cols_in, rows_in)
 
     def corners_of(k):
         return [
@@ -601,11 +626,10 @@
     calm = jnp.where(inside, extended[3], 0.0) - COURANT * (
         shifted(deep * flow[0], 0) + shifted(deep * flow[1], 1)
     )
-    for copies in (trace_copies, field_copies):
-        sent_all(copies)
-
-    own_side.wait()
-    received_all(side_copies)
+    sent(TRACES, traces_out.at[0 : peer_total - slots, :], traces_out.at[0:edge_slots, :])
+    sent(FIELDS, cols_out, rows_out)
+
+    received(SIDES, sides_in, None)
     beside = []
     last_turn = LANES - RIM * (CAP - 1)
     for shift, keep in (
@@ -619,9 +643,8 @@
     beside_hi, beside_lo = split(jnp.concatenate(beside, 0))
     side = mm(land_side, jnp.concatenate([beside_hi, beside_lo], 0))
 
-    own_items.wait()
-    received_all(item_copies)
-    received_all(edge_copies)
+    received(ITEMS, items_in, None)
+    received(RIMS, None, rims_in.at[0])
     deposit = mm(land, jnp.concatenate(split(items_in[...]), 0))
     bottom = []
     for i in (0, 1):
@@ -657,8 +680,9 @@
     sea_out[...] = level[0:tile_rows, 0:tile_cols]
     flow_out[0] = flow[0][0:tile_rows, 0:tile_cols]
     flow_out[1] = flow[1][0:tile_rows, 0:tile_cols]
-    for copies in (edge_copies, item_copies, side_copies):
-        sent_all(copies)
+    sent(RIMS, None, rims_out.at[0])
+    sent(ITEMS, items_out.at[0 : item_slots - CAP, :], None)
+    sent(SIDES, sides_out.at[0 : sub_count - 1], None)
 
 
 def store_kernel(new_in, sea_in, flow_in, new_out, sea_out, flow_out, sems):
@@ -718,7 +742,7 @@
         vmem((padded, padded), BF16),
         vmem((2 * send_total, 4 * elements), BF16),
         vmem((4 * FACE_ROWS, LANES), F32),
-        vmem((4 * FACE_ROWS, basis), F32),
+        vmem((4 * FACE_ROWS, LANES), F32),
         vmem((send_total, trace_lanes), F32),
         vmem((send_total, trace_lanes), F32),
         vmem((item_slots, cols), F32),
@@ -732,17 +756,11 @@
         vmem((2, sub_count, RIM, cols), F32),
         vmem((sub_count, 1, LANES), F32),
         vmem((sub_count, 1, LANES), F32),
+        vmem((item_slots + 2 * sub_count * RIM, cols), F32),
+        vmem((4 * trace_lanes, cols), BF16),
+        vmem((4 * trace_lanes, cols), BF16),
         dma((len(operands),)),
-        dma((8,)),
-        dma((8,)),
-        dma((sub_count + 2,)),
-        dma((sub_count + 2,)),
-        dma((sub_count,)),
-        dma((sub_count,)),
-        dma((sub_count,)),
-        dma((sub_count,)),
-        dma((2, sub_count)),
-        dma((2, sub_count)),
+        dma((15,)),
     ]
     hbm, local = pl.BlockSpec(memory_space=pltpu.HBM), pl.BlockSpec(memory_space=pltpu.VMEM)
     shapes = ((width, elements), (rows, cols), (2, rows, cols))

time: 28.1 us -> 26.7 us (0.950)
  Pallas kernels: 27.2 us -> 25.7 us
    pallas_call x1, Pallas kernels: 26.4 us -> 24.9 us  [body(): pl.pallas_call(functools.partial(kernel, mesh_count, sub_count), out_shap...]
where the time goes in v5:
time: 26.7 us; the launch traced here: 26.4 us
  Pallas kernels  25.7 us (96%)
  between operations  0.65 us (2%)
    pallas_call x1, Pallas kernels, body(): pl.pallas_call(functools.partial(kernel, mesh_count, sub_count), out_shap...  24.9 us
    pallas_call x1, Pallas kernels, body(): pl.pallas_call(store_kernel, out_shape=tuple((pltpu.HBM(shape, F32) for s...  0.79 us

profile of v5, /device:TPU:1, one launch (start us, length us, event | category | flops | bytes accessed | tf_op | source)
XLA Modules:
  0.0 26.4 jit_solution(16029919256556132219)
XLA Ops:
  0.6 24.9 %shard_map.202 = (f32[504,128]{1,0:T(8,128)S(1)}, f32[64,256]{1,0:T(8,128)S(1)}, f32[2,64,256]{2,1,0:T(8,128)S(1)}) custom-call(f32[504,128]{1,0:T(8,128)} %bitcast.19, f32[1,128]{1,0:T(1,128)} %bitcast.28, f32[168,56]{1,0:T(8,128)} %bitcast.20, f32[9,3,9]{2,1,0:T(4,128)} %bitcast.23, f32[21,4,56]{2,1,0:T(4,128)} %bitcast.21, f32[21,4,56]{2,1,0:T(4,128)} %bitcast.22, ...), custom_call_target="tpu_custom_call" | custom-call | tf_op jit(solution)/shard_map/pallas_call | solution.py:767
  25.6 0.8 %shard_map.203 = (f32[504,128]{1,0:T(8,128)}, f32[64,256]{1,0:T(8,128)}, f32[2,64,256]{2,1,0:T(8,128)}) custom-call(f32[504,128]{1,0:T(8,128)S(1)} %get-tuple-element.9.new_in, f32[64,256]{1,0:T(8,128)S(1)} %get-tuple-element.10.sea_in, f32[2,64,256]{2,1,0:T(8,128)S(1)} %get-tuple-element.11.flow_in), custom_call_target="tpu_custom_call" | custom-call | tf_op jit(solution)/shard_map/pallas_call | solution.py:777

commit v6 on v5

--- a/solution.py
+++ b/solution.py
@@ -17,7 +17,8 @@
 FACE_ROWS = 24
 INFO = 224
 RIM = 4
-TRACES, FIELDS, RIMS, ITEMS, SIDES = range(5)
+TRACES, FIELDS, RIMS, SIDES = range(4)
+ITEMS = RIMS
 TURN_LOW, TURN_HIGH = 1, 2
 DIRECTIONS = ((1, 0), (-1, 0), (0, 1), (0, -1), (1, 1), (1, -1), (-1, 1), (-1, -1))
 WAY = {d: i for i, d in enumerate(DIRECTIONS)}
@@ -120,33 +121,46 @@
     def device(dm, ds):
         return (me + dm, lax.rem(sub + ds + sub_count, sub_count))
 
-    loads = [
-        pltpu.make_async_copy(src, dst, load_sem.at[i])
-        for i, (src, dst) in enumerate(
-            (
-                (stiff_in, stiff), (jac_in, jac), (state_in, state), (scales_in, scales),
-                (psend_in, psend), (precv_in, precv), (esend_in, esend), (erecv_in, erecv),
-                (proj_in, proj), (felem_in, felem), (fdest_in, fdest), (frow_in, frow),
-                (fslip_in, fslip), (flux_in, flux), (lift_in, lift),
-                (vel_in, vel), (depth_in, depth), (uplift_in, uplift), (sea_in, sea),
-            )
-        )
-    ]
-    for load in loads:
-        load.start()
+    def loading(first, pairs):
+        return [
+            pltpu.make_async_copy(src, dst, load_sem.at[first + i])
+            for i, (src, dst) in enumerate(pairs)
+        ]
+
+    loads = loading(
+        0,
+        (
+            (stiff_in, stiff), (jac_in, jac), (state_in, state), (scales_in, scales),
+            (psend_in, psend), (precv_in, precv), (esend_in, esend), (erecv_in, erecv),
+            (proj_in, proj), (fdest_in, fdest), (frow_in, frow),
+        ),
+    )
+    late_loads = loading(
+        3,
+        (
+            (vel_in, vel), (depth_in, depth), (sea_in, sea), (uplift_in, uplift),
+            (lift_in, lift), (flux_in, flux), (felem_in, felem), (fslip_in, fslip),
+        ),
+    )
     barrier = pltpu.get_barrier_semaphore()
 
     def greet(dm, ds):
         pl.semaphore_signal(barrier, inc=1, device_id=device(dm, ds), device_id_type=MESH)
 
-    for k in range(1, sub_count):
+    order = sorted(range(1, sub_count), key=lambda k: -min(k, sub_count - k))
+    for k in order:
         greet(0, k)
+    for load in loads[0:4]:
+        load.start()
     for side in (1, -1):
 
         @pl.when(neighbour[side])
         def _():
-            for ds in range(sub_count):
+            for ds in [*order, 0]:
                 greet(side, ds)
+
+    for load in loads[4:]:
+        load.start()
 
     def start(group, copies):
         for side in (0, 1, -1):
@@ -193,19 +207,27 @@
     lane = iota((1, padded), 1)
     of_quantity = sum((lane >= basis * k).astype(I32) for k in range(1, quantities + 1))
     of_basis = lane - basis * of_quantity
-    spread_basis = (iota((basis, padded), 0) == of_basis).astype(F32).astype(BF16)
-    spread_quantity = (iota((quantities, padded), 0) == of_quantity).astype(F32)
-    for load in loads[0:15]:
+    half_row = iota((LANES, padded), 0) & (LANES // 2 - 1)
+    spread_basis = ((half_row == of_basis) & (lane < width)).astype(F32).astype(BF16)
+    spread_quantity = ((iota((48, padded), 0) & 15) == of_quantity).astype(F32).astype(BF16)
+    for load in loads:
         load.wait()
-    stiff_hi, stiff_lo = split(stiff[...])
-    spread[...] = mm(stiff_hi, spread_basis) + mm(stiff_lo, spread_basis)
-    jac_wide = [
-        lax.dot_general(
-            jac[:, d, :], spread_quantity, (((0,), (0,)), ((), ())),
-            precision=lax.Precision.HIGHEST, preferred_element_type=F32,
-        )
-        for d in range(3)
-    ]
+    for load in late_loads:
+        load.start()
+    stiff_hi, stiff_lo = split(
+        jnp.concatenate([stiff[...], jnp.zeros((3 * basis, LANES // 2 - basis), F32)], 1)
+    )
+    spread[...] = mm(
+        jnp.concatenate([stiff_hi, stiff_lo], 1), spread_basis
+    )
+    jac_wide = []
+    for d in range(3):
+        rest, jac_parts = jnp.concatenate([jac[:, d, :], jnp.zeros((16 - quantities, quantities), F32)], 0), []
+        for _ in range(3):
+            part = rest.astype(BF16)
+            rest = rest - part.astype(F32)
+            jac_parts.append(part)
+        jac_wide.append(mm(jnp.concatenate(jac_parts, 0), spread_quantity, 0, 0))
 
     def matrix_rows(q):
         if q == quantities:
@@ -303,19 +325,24 @@
         [jnp.concatenate([face_block(f, q) for q in range(quantities)], 0) for f in range(4)], 1
     )
     table = jnp.concatenate([table, jnp.zeros((trace_rows - face_width, 4 * elements), F32)], 0)
-    table_hi, table_lo = split(table)
-    picked = mm(hot[...], table_hi, 1, 1) + mm(hot[...], table_lo, 1, 1)
-    traces_out[:, 0:LANES] = picked[0:send_total, 0:LANES]
-    traces_out[0:peer_total, LANES:] = jnp.where(
-        info_here, info, picked[0:peer_total, LANES:]
-    )
-    traces_out[peer_total:, LANES:] = picked[peer_total:send_total, LANES:]
-    own_trace = picked[send_total:]
+    deep_half = 2 * elements
+    tables = [split(table[:, 0:deep_half]), split(table[:, deep_half:])]
+
+    def pick(rows):
+        return sum(
+            mm(hot[rows, i * deep_half : (i + 1) * deep_half], part, 1, 1)
+            for i in (0, 1)
+            for part in tables[i]
+        )
+
+    picked = pick(slice(0, send_total))
+    traces_out[:, 0:LANES] = picked[:, 0:LANES]
+    traces_out[0:peer_total, LANES:] = jnp.where(info_here, info, picked[0:peer_total, LANES:])
+    traces_out[peer_total:, LANES:] = picked[peer_total:, LANES:]
 
     def peer_block(index, rows):
         return pl.ds(pl.multiple_of(index * rows, rows), rows)
 
-    order = sorted(range(1, sub_count), key=lambda k: -min(k, sub_count - k))
     trace_copies = []
     for k in order:
         _, peer = device(0, k)
@@ -344,7 +371,9 @@
         TRACES, traces_out.at[peer_block(sub, slots), :], traces_in.at[peer_block(sub, slots), :]
     )
 
-    for load in loads[15:]:
+    own_trace = pick(slice(send_total, 2 * send_total))
+
+    for load in late_loads:
         load.wait()
     for i, first in enumerate((tile_rows - 8, 0)):
         rows_out[i, 0:2] = vel[:, first : first + 8, :]
@@ -494,9 +523,9 @@
     diff_hi, diff_lo = split(difference)
     turned_hi = jnp.concatenate([diff_hi * turn for turn in turns], 1)
     turned_lo = jnp.concatenate([diff_lo * turn for turn in turns], 1)
-    each_hi, each_lo = split(
-        mm(turned_hi, mixing_hi[...]) + mm(turned_lo, mixing_hi[...]) + mm(turned_hi, mixing_lo[...])
-    )
+    each = mm(jnp.concatenate([turned_hi, turned_lo], 0), mixing_hi[...])
+    each = each[:send_total] + each[send_total:] + mm(turned_hi, mixing_lo[...])
+    each_hi, each_lo = split(each)
     uplifted = known[...] + mm(touch, jnp.concatenate([each_hi, each_lo], 0))
     uplifted = jnp.concatenate(
         [uplifted[:item_slots], uplifted[item_slots:] + mm(touch_lo, each_hi)], 0
@@ -629,23 +658,7 @@
     sent(TRACES, traces_out.at[0 : peer_total - slots, :], traces_out.at[0:edge_slots, :])
     sent(FIELDS, cols_out, rows_out)
 
-    received(SIDES, sides_in, None)
-    beside = []
-    last_turn = LANES - RIM * (CAP - 1)
-    for shift, keep in (
-        (last_turn, side_lane < RIM - 1),
-        (last_turn + LANES // 2 - RIM + 1, side_lane > LANES - RIM),
-    ):
-        for s in range(sub_count):
-            wide = jnp.broadcast_to(sides_in[s], (CAP, LANES))
-            wide = pltpu.roll(wide, shift % LANES, 1, stride=RIM, stride_axis=0)
-            beside.append(jnp.where(keep, wide, 0.0))
-    beside_hi, beside_lo = split(jnp.concatenate(beside, 0))
-    side = mm(land_side, jnp.concatenate([beside_hi, beside_lo], 0))
-
-    received(ITEMS, items_in, None)
     received(RIMS, None, rims_in.at[0])
-    deposit = mm(land, jnp.concatenate(split(items_in[...]), 0))
     bottom = []
     for i in (0, 1):
         total = rims_in[i, 0]
@@ -668,6 +681,21 @@
             around.append(rows)
         corner.append(jnp.where(bottom_lane < LANES // 2, around[0], around[1]))
     corner = jnp.where(bottom_row < RIM, corner[0], corner[1])
+    received(SIDES, sides_in, None)
+    received(ITEMS, items_in, None)
+    beside = []
+    last_turn = LANES - RIM * (CAP - 1)
+    for shift, keep in (
+        (last_turn, side_lane < RIM - 1),
+        (last_turn + LANES // 2 - RIM + 1, side_lane > LANES - RIM),
+    ):
+        for s in range(sub_count):
+            wide = jnp.broadcast_to(sides_in[s], (CAP, LANES))
+            wide = pltpu.roll(wide, shift % LANES, 1, stride=RIM, stride_axis=0)
+            beside.append(jnp.where(keep, wide, 0.0))
+    beside_hi, beside_lo = split(jnp.concatenate(beside, 0))
+    side = mm(land_side, jnp.concatenate([beside_hi, beside_lo], 0))
+    deposit = mm(land, jnp.concatenate(split(items_in[...]), 0))
     raised = jnp.concatenate(
         [jnp.concatenate([deposit, side], 1), jnp.concatenate([bottom, corner], 1)], 0
     )
@@ -759,8 +787,8 @@
         vmem((item_slots + 2 * sub_count * RIM, cols), F32),
         vmem((4 * trace_lanes, cols), BF16),
         vmem((4 * trace_lanes, cols), BF16),
-        dma((len(operands),)),
-        dma((15,)),
+        dma((11,)),
+        dma((10,)),
     ]
     hbm, local = pl.BlockSpec(memory_space=pltpu.HBM), pl.BlockSpec(memory_space=pltpu.VMEM)
     shapes = ((width, elements), (rows, cols), (2, rows, cols))

time: 26.7 us -> 26.6 us (level)
  no operation moved by 1% of the time
where the time goes in v6:
time: 26.6 us; the launch traced here: 26.4 us
  Pallas kernels  25.8 us (97%)
  between operations  0.65 us (2%)
    pallas_call x1, Pallas kernels, body(): pl.pallas_call(functools.partial(kernel, mesh_count, sub_count), out_shap...  25 us
    pallas_call x1, Pallas kernels, body(): pl.pallas_call(store_kernel, out_shape=tuple((pltpu.HBM(shape, F32) for s...  0.79 us

profile of v6, /device:TPU:1, one launch (start us, length us, event | category | flops | bytes accessed | tf_op | source)
XLA Modules:
  0.0 26.4 jit_solution(9948622943885676281)
XLA Ops:
  0.6 25.0 %shard_map.202 = (f32[504,128]{1,0:T(8,128)S(1)}, f32[64,256]{1,0:T(8,128)S(1)}, f32[2,64,256]{2,1,0:T(8,128)S(1)}) custom-call(f32[504,128]{1,0:T(8,128)} %bitcast.19, f32[1,128]{1,0:T(1,128)} %bitcast.28, f32[168,56]{1,0:T(8,128)} %bitcast.20, f32[9,3,9]{2,1,0:T(4,128)} %bitcast.23, f32[21,4,56]{2,1,0:T(4,128)} %bitcast.21, f32[21,4,56]{2,1,0:T(4,128)} %bitcast.22, ...), custom_call_target="tpu_custom_call" | custom-call | tf_op jit(solution)/shard_map/pallas_call | solution.py:795
  25.6 0.8 %shard_map.203 = (f32[504,128]{1,0:T(8,128)}, f32[64,256]{1,0:T(8,128)}, f32[2,64,256]{2,1,0:T(8,128)}) custom-call(f32[504,128]{1,0:T(8,128)S(1)} %get-tuple-element.9.new_in, f32[64,256]{1,0:T(8,128)S(1)} %get-tuple-element.10.sea_in, f32[2,64,256]{2,1,0:T(8,128)S(1)} %get-tuple-element.11.flow_in), custom_call_target="tpu_custom_call" | custom-call | tf_op jit(solution)/shard_map/pallas_call | solution.py:805
